TPU v7x, 32 devices: a whole 2x2x4 slice. The times are simulated.
32 devices in a mesh: scene: 2 (over y), gx: 4 (over z), gy: 4 (over x, core).
Axes of the slice: x: 2, y: 2, z: 4, core: 2. Of those that a mesh axis runs over, the one named last changes fastest.
Arguments:
- feats: bfloat16 [64, 96, 512], P(('scene', 'gx', 'gy')), parts along dimension 0
- voxel_mask: int32 [64, 512], P(('scene', 'gx', 'gy')), parts along dimension 0, may hold values 0 or 1
- block_slot: int32 [64], P(('scene', 'gx', 'gy')), parts along dimension 0, may hold values from 0 to 3, as said below
- block_count: int32 [32], P(('scene', 'gx', 'gy')), parts along dimension 0, may hold values from 1 to 2, as said below
- weight_one: bfloat16 [96, 2592], replicated, may hold values from -0.125 to 0.125
- weight_two: bfloat16 [96, 2592], replicated, may hold values from -0.125 to 0.125
- gain_one: float32 [96], replicated, may hold values from 0.5 to 1.5
- shift_one: float32 [96], replicated, may hold values from -3 to 3
- gain_two: float32 [96], replicated, may hold values from 0.5 to 1.5
- shift_two: float32 [96], replicated, may hold values from -3 to 3
- cotangent: bfloat16 [64, 96, 512], P(('scene', 'gx', 'gy')), parts along dimension 0, may hold values from -6 to 6
Outputs:
- output: bfloat16 [64, 96, 512], P(('scene', 'gx', 'gy')), parts along dimension 0
- feats_grad: bfloat16 [64, 96, 512], P(('scene', 'gx', 'gy')), parts along dimension 0
- weight_grad_one: float32 [192, 2592], P('scene'), parts along dimension 0
- weight_grad_two: float32 [192, 2592], P('scene'), parts along dimension 0
- norm_grads: float32 [8, 96], P('scene'), parts along dimension 0
There are 2 independent parts, one for each index of `scene`. A program takes and returns all parts, laid end to end along the dimension named above; an argument that names none is the same for every part. Nothing has to cross between parts.
Inputs may be any that keep to these rules, and one draw needn't show every extreme that they name: `block_slot`: the 2 entries of one device name distinct slots of its 4 region slots. `block_count`: some device of every scene has all 2 entries live.
All inputs are finite; a program needn't handle non-finite values. No bound on the sum of `voxel_mask` on one device may be relied on, other than what follows from the above.
Results may differ from a plain program's by a relative error of at most 0.0061.
Values may be sent and summed in bfloat16 or wider, within the bound.
A program may use at most 64 MiB of HBM per device.

v0:
```python
import jax
import jax.numpy as jnp
from jax import lax
from jax.sharding import PartitionSpec as P

EPS = 1e-05


def extended(array, sides, width):
    for axis, dim in sides:
        size, length = (lax.axis_size(axis), array.shape[dim])
        up = [(i, (i + 1) % size) for i in range(size - 1)]
        down = [(j, i) for i, j in up]
        last = lax.slice_in_dim(array, length - width, length, axis=dim)
        leading = lax.slice_in_dim(array, 0, width, axis=dim)
        before = lax.ppermute(last, axis, up)
        after = lax.ppermute(leading, axis, down)
        array = jnp.concatenate([before, array, after], axis=dim)
    return array


def unfold(window):
    channels = window.shape[0]
    pieces = []
    for step_x in range(3):
        for step_y in range(3):
            for step_z in range(3):
                pieces.append(
                    window[
                        :, step_x : step_x + 8, step_y : step_y + 8, step_z : step_z + 8
                    ].reshape(channels, 512)
                )
    return jnp.concatenate(pieces, axis=0)


def flipped(weight):
    channels = weight.shape[0]
    return (
        jnp.flip(weight.reshape(channels, 27, channels), axis=1)
        .transpose(2, 1, 0)
        .reshape(channels, 27 * channels)
    )


def silu_slope(values):
    sigma = jax.nn.sigmoid(values)
    return sigma * (1.0 + values * (1.0 - sigma))


def region_field(blocks, block_slot):
    slots_here, channels = (blocks.shape[0], blocks.shape[1])
    layers = slots_here // 2
    onehot = (block_slot[:, None] == jnp.arange(4 * layers, dtype=jnp.int32)[None, :]).astype(
        blocks.dtype
    )
    placed = jnp.einsum("ks,kcv->scv", onehot, blocks, preferred_element_type=jnp.float32).astype(
        blocks.dtype
    )
    placed = placed.reshape(2, 2, layers, channels, 8, 8, 8).transpose(3, 0, 4, 1, 5, 2, 6)
    placed = placed.reshape(channels, 16, 16, 8 * layers)
    padded = extended(placed, (("gx", 1), ("gy", 2)), 1)
    return jnp.pad(padded, ((0, 0), (0, 0), (0, 0), (1, 1)))


def block_window(padded, corner):
    channels = padded.shape[0]
    start = (jnp.zeros((), jnp.int32), corner[0] * 8, corner[1] * 8, corner[2] * 8)
    return unfold(lax.dynamic_slice(padded, start, (channels, 10, 10, 10)))


def apply_kernel(weight, padded, corners):

    def one_block(corner):
        return jnp.dot(weight, block_window(padded, corner), preferred_element_type=jnp.float32)

    return lax.map(one_block, corners)


def kernel_grad(grad, padded, corners):
    channels = grad.shape[1]

    def add_block(total, item):
        corner, piece = item
        columns = block_window(padded, corner)
        return (
            total
            + lax.dot_general(
                piece, columns, (((1,), (1,)), ((), ())), preferred_element_type=jnp.float32
            ),
            None,
        )

    total, _ = lax.scan(
        add_block, jnp.zeros((channels, 27 * channels), jnp.float32), (corners, grad)
    )
    return total


def norm_forward(values, mask, gain, shift):
    total, square, count = lax.psum(
        (jnp.sum(values, axis=(0, 2)), jnp.sum(values * values, axis=(0, 2)), jnp.sum(mask)),
        ("gx", "gy"),
    )
    mean = total / count
    var = square / count - mean * mean
    centred = (values - mean[None, :, None]) * mask[:, None, :]
    inv_std = lax.rsqrt(var + EPS)
    normed = centred * inv_std[None, :, None]
    return (normed, normed * gain[None, :, None] + shift[None, :, None], inv_std, count)


def norm_back(grad_z, normed, gain, inv_std, mask, count):
    shift_grad, gain_grad = lax.psum(
        (jnp.sum(grad_z, axis=(0, 2)), jnp.sum(grad_z * normed, axis=(0, 2))), ("gx", "gy")
    )
    scaled = (gain * inv_std)[None, :, None]
    grad = (
        mask[:, None, :]
        * scaled
        * (grad_z - shift_grad[None, :, None] / count - normed * gain_grad[None, :, None] / count)
    )
    return (grad.astype(jnp.bfloat16), gain_grad, shift_grad)


def per_device(
    feats,
    voxel_mask,
    block_slot,
    block_count,
    weight_one,
    weight_two,
    gain_one,
    shift_one,
    gain_two,
    shift_two,
    cotangent,
):
    slots_here = feats.shape[0]
    layers = slots_here // 2
    valid = jnp.arange(slots_here, dtype=jnp.int32) < block_count[0]
    mask = voxel_mask.astype(jnp.float32) * valid.astype(jnp.float32)[:, None]
    corners = jnp.stack(
        [block_slot // (2 * layers), block_slot // layers % 2, block_slot % layers], axis=1
    )
    inputs = feats * mask[:, None, :].astype(jnp.bfloat16)
    input_field = region_field(inputs, block_slot)
    conv_one = apply_kernel(weight_one, input_field, corners) * mask[:, None, :]
    normed_one, shifted_one, inv_one, count = norm_forward(conv_one, mask, gain_one, shift_one)
    active = (jax.nn.silu(shifted_one) * mask[:, None, :]).astype(jnp.bfloat16)
    active_field = region_field(active, block_slot)
    conv_two = apply_kernel(weight_two, active_field, corners) * mask[:, None, :]
    normed_two, shifted_two, inv_two, count = norm_forward(conv_two, mask, gain_two, shift_two)
    output = (jax.nn.silu(shifted_two) * mask[:, None, :]).astype(jnp.bfloat16)
    grad_z2 = cotangent.astype(jnp.float32) * mask[:, None, :] * silu_slope(shifted_two)
    grad_y2, gain_grad_two, shift_grad_two = norm_back(
        grad_z2, normed_two, gain_two, inv_two, mask, count
    )
    partial_two = kernel_grad(grad_y2, active_field, corners)
    total_two = lax.psum(partial_two, ("gx", "gy"))
    grad_a1 = apply_kernel(flipped(weight_two), region_field(grad_y2, block_slot), corners)
    grad_z1 = grad_a1 * mask[:, None, :] * silu_slope(shifted_one)
    grad_y1, gain_grad_one, shift_grad_one = norm_back(
        grad_z1, normed_one, gain_one, inv_one, mask, count
    )
    partial_one = kernel_grad(grad_y1, input_field, corners)
    feats_grad = (
        apply_kernel(flipped(weight_one), region_field(grad_y1, block_slot), corners)
        * mask[:, None, :]
    ).astype(jnp.bfloat16)
    total_one = lax.psum(partial_one, ("gx", "gy"))
    norm_grads = jnp.stack([gain_grad_one, shift_grad_one, gain_grad_two, shift_grad_two])
    return (output, feats_grad, total_one, total_two, norm_grads)


def solution(mesh):
    placed = (
        P(("scene", "gx", "gy"), None, None),
        P(("scene", "gx", "gy"), None),
        P(("scene", "gx", "gy")),
        P(("scene", "gx", "gy")),
        P(),
        P(),
        P(),
        P(),
        P(),
        P(),
        P(("scene", "gx", "gy"), None, None),
    )
    return jax.shard_map(
        per_device,
        mesh=mesh,
        in_specs=placed,
        out_specs=(
            P(("scene", "gx", "gy"), None, None),
            P(("scene", "gx", "gy"), None, None),
            P("scene", None),
            P("scene", None),
            P("scene", None),
        ),
        check_vma=False,
    )
```

profile of v0, /device:TPU:0, one launch (start us, length us, event | category | flops | bytes accessed | tf_op | source)
XLA Modules:
  0.0 464.4 jit_solution(16859884598967300127)
XLA Ops:
  11.8 4.9 %collective-permute-start = (bf16[96,1,16,8]{0,3,2,1:T(8,128)(2,1)S(1)}, bf16[96,1,16,8]{0,3,2,1:T(8,128)(2,1)S(1)}, u32[]{:S(2)}, u32[]{:S(2)}) collective-permute-start(bf16[96,1,16,8]{0,3,2,1:T(8,128)(2,1)S(1)} %get-tuple-element.576), channel_id=1, source_target_pairs={{0,4},{4,8},{8,12},{1,5},{5,9},{9,13},{2,6},{6,10},{10,14},{3,7},{... | collective-permute-start | bytes 73736 | tf_op jit(solution)/shard_map/ppermute | solution.py:16
  18.4 4.2 collective-permute-done.1
  30.3 26.3 %while.62 = (s32[]{:T(128)}, f32[2,96,512]{2,1,0:T(8,128)}, s32[2,3]{1,0:T(2,128)S(1)}, bf16[96,18,18,10]{0,3,2,1:T(8,128)(2,1)S(1)}, bf16[96,2592]{1,0:T(8,128)...) while((s32[]{:T(128)}, f32[2,96,512]{2,1,0:T(8,128)}, ...), condition=%wide.region_1.2_spmd, body=%wide.region_0.1_spmd.sunk | while | flops 254803984 | bytes 14064725 | solution.py:76
  34.1 5.9 %concatenate.58 = bf16[2592,512]{0,1:T(8,128)(2,1)} concatenate(bf16[96,512]{0,1:T(8,128)(2,1)} %bitcast.664, bf16[96,512]{0,1:T(8,128)(2,1)} %bitcast.663, bf16[96,512]{0,1:T(8,128)(2,1)} %bitcast.662, bf16[96,512]{0,1:T(8,128)(2,1)} %bitcast.661, bf16[96,512]{0,1:T(8,128)(2,1)} %bitcast.660, bf16[96,512]{0,1:T(8,128)(2,1)} %bitcast.659, bf16[96,512]{0,1:T(8,128)(2,1)} %bitcast.658, ...), dimensions={0} | concatenate | bytes 5308416 | tf_op jit(solution)/shard_map/while/body/eval_jaxpr/concatenate | solution.py:33
  40.0 3.4 fusion.89
  47.3 5.9 %concatenate.58 = bf16[2592,512]{0,1:T(8,128)(2,1)} concatenate(bf16[96,512]{0,1:T(8,128)(2,1)} %bitcast.664, bf16[96,512]{0,1:T(8,128)(2,1)} %bitcast.663, bf16[96,512]{0,1:T(8,128)(2,1)} %bitcast.662, bf16[96,512]{0,1:T(8,128)(2,1)} %bitcast.661, bf16[96,512]{0,1:T(8,128)(2,1)} %bitcast.660, bf16[96,512]{0,1:T(8,128)(2,1)} %bitcast.659, bf16[96,512]{0,1:T(8,128)(2,1)} %bitcast.658, ...), dimensions={0} | concatenate | bytes 5308416 | tf_op jit(solution)/shard_map/while/body/eval_jaxpr/concatenate | solution.py:33
  53.2 3.4 fusion.89
  57.8 32.7 %all-reduce.7 = (f32[96]{0:T(128)S(1)}, f32[]{:T(128)}, f32[96]{0:T(128)S(1)}) all-reduce(f32[96]{0:T(128)S(1)} %get-tuple-element.302, f32[]{:T(128)} %get-tuple-element.386, f32[96]{0:T(128)S(1)} %get-tuple-element.301), channel_id=1, replica_groups=mesh['scene'=2,'gx'=4,'gy'=4] {'gx','gy'}, use_global_device_ids=true, to_apply=%region_3.4 | all-reduce | flops 193 | bytes 1544 | tf_op jit(solution)/shard_map/psum | solution.py:100
  111.9 26.9 %while.63 = (s32[]{:T(128)}, f32[2,96,512]{2,1,0:T(8,128)}, s32[2,3]{1,0:T(2,128)S(1)}, bf16[96,18,18,10]{0,3,2,1:T(8,128)(2,1)S(1)}, bf16[96,2592]{1,0:T(8,128)...) while((s32[]{:T(128)}, f32[2,96,512]{2,1,0:T(8,128)}, ...), condition=%wide.region_9.10_spmd, body=%wide.region_8.9_spmd.sunk | while | flops 254803984 | bytes 14064477 | solution.py:76
  115.9 6.1 %concatenate.59 = bf16[2592,512]{0,1:T(8,128)(2,1)} concatenate(bf16[96,512]{0,1:T(8,128)(2,1)} %bitcast.691, bf16[96,512]{0,1:T(8,128)(2,1)} %bitcast.690, bf16[96,512]{0,1:T(8,128)(2,1)} %bitcast.689, bf16[96,512]{0,1:T(8,128)(2,1)} %bitcast.688, bf16[96,512]{0,1:T(8,128)(2,1)} %bitcast.687, bf16[96,512]{0,1:T(8,128)(2,1)} %bitcast.686, bf16[96,512]{0,1:T(8,128)(2,1)} %bitcast.685, ...), dimensions={0} | concatenate | bytes 5308416 | tf_op jit(solution)/shard_map/while/body/eval_jaxpr/concatenate | solution.py:33
  129.4 6.1 %concatenate.59 = bf16[2592,512]{0,1:T(8,128)(2,1)} concatenate(bf16[96,512]{0,1:T(8,128)(2,1)} %bitcast.691, bf16[96,512]{0,1:T(8,128)(2,1)} %bitcast.690, bf16[96,512]{0,1:T(8,128)(2,1)} %bitcast.689, bf16[96,512]{0,1:T(8,128)(2,1)} %bitcast.688, bf16[96,512]{0,1:T(8,128)(2,1)} %bitcast.687, bf16[96,512]{0,1:T(8,128)(2,1)} %bitcast.686, bf16[96,512]{0,1:T(8,128)(2,1)} %bitcast.685, ...), dimensions={0} | concatenate | bytes 5308416 | tf_op jit(solution)/shard_map/while/body/eval_jaxpr/concatenate | solution.py:33
  140.1 30.7 %all-reduce.6 = (f32[96]{0:T(128)S(1)}, f32[96]{0:T(128)S(1)}) all-reduce(f32[96]{0:T(128)S(1)} %get-tuple-element.300, f32[96]{0:T(128)S(1)} %get-tuple-element.299), channel_id=1, replica_groups=mesh['scene'=2,'gx'=4,'gy'=4] {'gx','gy'}, use_global_device_ids=true, to_apply=%region_11.12 | all-reduce | flops 192 | bytes 1536 | tf_op jit(solution)/shard_map/psum | solution.py:100
  173.9 29.5 %all-reduce.5 = (f32[96]{0:T(128)S(1)}, f32[96]{0:T(128)S(1)}) all-reduce(f32[96]{0:T(128)S(1)} %get-tuple-element.306, f32[96]{0:T(128)S(1)} %get-tuple-element.305), channel_id=1, replica_groups=mesh['scene'=2,'gx'=4,'gy'=4] {'gx','gy'}, use_global_device_ids=true, to_apply=%region_17.18 | all-reduce | flops 192 | bytes 1536 | tf_op jit(solution)/shard_map/psum | solution.py:113
  226.2 27.8 %while.67 = (s32[]{:T(128)}, f32[96,2592]{1,0:T(8,128)}, bf16[2,96,512]{2,1,0:T(8,128)(2,1)}, s32[2,3]{1,0:T(2,128)S(1)}, bf16[96,18,18,10]{0,3,2,1:T(8,128)(2,1...) while((s32[]{:T(128)}, f32[96,2592]{1,0:T(8,128)}, ...), condition=%wide.region_30.31_spmd.clone, body=%wide.region_29.30_spmd.clone.sunk | while | flops 255301648 | bytes 15496287 | solution.py:93
  230.5 6.1 %concatenate.63 = bf16[2592,512]{0,1:T(8,128)(2,1)} concatenate(bf16[96,512]{0,1:T(8,128)(2,1)} %bitcast.718, bf16[96,512]{0,1:T(8,128)(2,1)} %bitcast.717, bf16[96,512]{0,1:T(8,128)(2,1)} %bitcast.716, bf16[96,512]{0,1:T(8,128)(2,1)} %bitcast.715, bf16[96,512]{0,1:T(8,128)(2,1)} %bitcast.714, bf16[96,512]{0,1:T(8,128)(2,1)} %bitcast.713, bf16[96,512]{0,1:T(8,128)(2,1)} %bitcast.712, ...), dimensions={0} | concatenate | bytes 5308416 | tf_op jit(solution)/shard_map/while/body/eval_jaxpr/concatenate | solution.py:33
  244.2 6.1 %concatenate.63 = bf16[2592,512]{0,1:T(8,128)(2,1)} concatenate(bf16[96,512]{0,1:T(8,128)(2,1)} %bitcast.718, bf16[96,512]{0,1:T(8,128)(2,1)} %bitcast.717, bf16[96,512]{0,1:T(8,128)(2,1)} %bitcast.716, bf16[96,512]{0,1:T(8,128)(2,1)} %bitcast.715, bf16[96,512]{0,1:T(8,128)(2,1)} %bitcast.714, bf16[96,512]{0,1:T(8,128)(2,1)} %bitcast.713, bf16[96,512]{0,1:T(8,128)(2,1)} %bitcast.712, ...), dimensions={0} | concatenate | bytes 5308416 | tf_op jit(solution)/shard_map/while/body/eval_jaxpr/concatenate | solution.py:33
  250.3 3.7 convolution_add_fusion.5
  256.7 27.0 %while.64 = (s32[]{:T(128)}, f32[2,96,512]{2,1,0:T(8,128)}, s32[2,3]{1,0:T(2,128)S(1)}, bf16[96,18,18,10]{0,3,2,1:T(8,128)(2,1)S(1)}, bf16[96,2592]{1,0:T(8,128)...) while((s32[]{:T(128)}, f32[2,96,512]{2,1,0:T(8,128)}, ...), condition=%wide.region_19.20_spmd, body=%wide.region_18.19_spmd.sunk | while | flops 254803984 | bytes 14083157 | solution.py:76
  260.6 6.1 %concatenate.60 = bf16[2592,512]{0,1:T(8,128)(2,1)} concatenate(bf16[96,512]{0,1:T(8,128)(2,1)} %bitcast.745, bf16[96,512]{0,1:T(8,128)(2,1)} %bitcast.744, bf16[96,512]{0,1:T(8,128)(2,1)} %bitcast.743, bf16[96,512]{0,1:T(8,128)(2,1)} %bitcast.742, bf16[96,512]{0,1:T(8,128)(2,1)} %bitcast.741, bf16[96,512]{0,1:T(8,128)(2,1)} %bitcast.740, bf16[96,512]{0,1:T(8,128)(2,1)} %bitcast.739, ...), dimensions={0} | concatenate | bytes 5308416 | tf_op jit(solution)/shard_map/while/body/eval_jaxpr/concatenate | solution.py:33
  266.7 3.5 fusion.97
  274.0 6.1 %concatenate.60 = bf16[2592,512]{0,1:T(8,128)(2,1)} concatenate(bf16[96,512]{0,1:T(8,128)(2,1)} %bitcast.745, bf16[96,512]{0,1:T(8,128)(2,1)} %bitcast.744, bf16[96,512]{0,1:T(8,128)(2,1)} %bitcast.743, bf16[96,512]{0,1:T(8,128)(2,1)} %bitcast.742, bf16[96,512]{0,1:T(8,128)(2,1)} %bitcast.741, bf16[96,512]{0,1:T(8,128)(2,1)} %bitcast.740, bf16[96,512]{0,1:T(8,128)(2,1)} %bitcast.739, ...), dimensions={0} | concatenate | bytes 5308416 | tf_op jit(solution)/shard_map/while/body/eval_jaxpr/concatenate | solution.py:33
  280.1 3.5 fusion.97
  286.1 32.9 %all-reduce.4 = (f32[96]{0:T(128)S(1)}, f32[96]{0:T(128)S(1)}) all-reduce(f32[96]{0:T(128)S(1)} %get-tuple-element.304, f32[96]{0:T(128)S(1)} %get-tuple-element.303), channel_id=1, replica_groups=mesh['scene'=2,'gx'=4,'gy'=4] {'gx','gy'}, use_global_device_ids=true, to_apply=%region_23.24 | all-reduce | flops 192 | bytes 1536 | tf_op jit(solution)/shard_map/psum | solution.py:113
  330.7 25.2 %while.66 = (s32[]{:T(128)}, f32[96,2592]{1,0:T(8,128)S(1)}, bf16[2,96,512]{2,1,0:T(8,128)(2,1)S(1)}, s32[2,3]{1,0:T(2,128)S(1)}, bf16[96,18,18,10]{0,3,2,1:T(8,...) while((s32[]{:T(128)}, f32[96,2592]{1,0:T(8,128)S(1)}, ...), condition=%wide.region_27.28_spmd.clone, body=%wide.region_26.27_spmd.clone.sunk | while | flops 255301648 | bytes 17032344 | solution.py:93
  334.7 6.0 %concatenate.62 = bf16[2592,512]{0,1:T(8,128)(2,1)} concatenate(bf16[96,512]{0,1:T(8,128)(2,1)} %bitcast.772, bf16[96,512]{0,1:T(8,128)(2,1)} %bitcast.771, bf16[96,512]{0,1:T(8,128)(2,1)} %bitcast.770, bf16[96,512]{0,1:T(8,128)(2,1)} %bitcast.769, bf16[96,512]{0,1:T(8,128)(2,1)} %bitcast.768, bf16[96,512]{0,1:T(8,128)(2,1)} %bitcast.767, bf16[96,512]{0,1:T(8,128)(2,1)} %bitcast.766, ...), dimensions={0} | concatenate | bytes 5308416 | tf_op jit(solution)/shard_map/while/body/eval_jaxpr/concatenate | solution.py:33
  347.3 6.0 %concatenate.62 = bf16[2592,512]{0,1:T(8,128)(2,1)} concatenate(bf16[96,512]{0,1:T(8,128)(2,1)} %bitcast.772, bf16[96,512]{0,1:T(8,128)(2,1)} %bitcast.771, bf16[96,512]{0,1:T(8,128)(2,1)} %bitcast.770, bf16[96,512]{0,1:T(8,128)(2,1)} %bitcast.769, bf16[96,512]{0,1:T(8,128)(2,1)} %bitcast.768, bf16[96,512]{0,1:T(8,128)(2,1)} %bitcast.767, bf16[96,512]{0,1:T(8,128)(2,1)} %bitcast.766, ...), dimensions={0} | concatenate | bytes 5308416 | tf_op jit(solution)/shard_map/while/body/eval_jaxpr/concatenate | solution.py:33
  365.6 30.7 %while.65 = (s32[]{:T(128)}, f32[2,96,512]{2,1,0:T(8,128)}, s32[2,3]{1,0:T(2,128)S(1)}, bf16[96,18,18,10]{0,3,2,1:T(8,128)(2,1)}, bf16[96,2592]{1,0:T(8,128)(2,1...) while((s32[]{:T(128)}, f32[2,96,512]{2,1,0:T(8,128)}, ...), condition=%wide.region_25.26_spmd, body=%wide.region_24.25_spmd.sunk | while | flops 254803984 | bytes 13966421 | solution.py:76
  367.4 6.6 %constant_dynamic-slice_fusion.187 = (bf16[96,8,8,8]{0,3,2,1:T(8,128)(2,1)S(1)}, bf16[96,8,8,8]{0,3,2,1:T(8,128)(2,1)S(1)}, bf16[96,8,8,8]{0,3,2,1:T(8,128)(2,1)...) fusion(bf16[96,18,18,10]{0,3,2,1:T(8,128)(2,1)} %get-tuple-elem, ...), kind=kLoop, calls=%fused_computation.118.clone.1 | loop fusion | bytes 5308448 | tf_op jit(solution)/shard_map/while/body/eval_jaxpr/slice | solution.py:29
  374.1 5.3 %concatenate.61 = bf16[2592,512]{0,1:T(8,128)(2,1)S(1)} concatenate(bf16[96,512]{0,1:T(8,128)(2,1)} %bitcast.799, bf16[96,512]{0,1:T(8,128)(2,1)} %bitcast.798, bf16[96,512]{0,1:T(8,128)(2,1)} %bitcast.797, bf16[96,512]{0,1:T(8,128)(2,1)} %bitcast.796, bf16[96,512]{0,1:T(8,128)(2,1)} %bitcast.795, bf16[96,512]{0,1:T(8,128)(2,1)} %bitcast.794, bf16[96,512]{0,1:T(8,128)(2,1)} %bitcast.793, ...), dimensions={0} | concatenate | bytes 5308416 | tf_op jit(solution)/shard_map/while/body/eval_jaxpr/concatenate | solution.py:33
  382.8 6.5 %constant_dynamic-slice_fusion.187 = (bf16[96,8,8,8]{0,3,2,1:T(8,128)(2,1)S(1)}, bf16[96,8,8,8]{0,3,2,1:T(8,128)(2,1)S(1)}, bf16[96,8,8,8]{0,3,2,1:T(8,128)(2,1)...) fusion(bf16[96,18,18,10]{0,3,2,1:T(8,128)(2,1)} %get-tuple-elem, ...), kind=kLoop, calls=%fused_computation.118.clone.1 | loop fusion | bytes 5308448 | tf_op jit(solution)/shard_map/while/body/eval_jaxpr/slice | solution.py:29
  389.4 5.3 %concatenate.61 = bf16[2592,512]{0,1:T(8,128)(2,1)S(1)} concatenate(bf16[96,512]{0,1:T(8,128)(2,1)} %bitcast.799, bf16[96,512]{0,1:T(8,128)(2,1)} %bitcast.798, bf16[96,512]{0,1:T(8,128)(2,1)} %bitcast.797, bf16[96,512]{0,1:T(8,128)(2,1)} %bitcast.796, bf16[96,512]{0,1:T(8,128)(2,1)} %bitcast.795, bf16[96,512]{0,1:T(8,128)(2,1)} %bitcast.794, bf16[96,512]{0,1:T(8,128)(2,1)} %bitcast.793, ...), dimensions={0} | concatenate | bytes 5308416 | tf_op jit(solution)/shard_map/while/body/eval_jaxpr/concatenate | solution.py:33
  398.0 56.2 %all-reduce.11.cloned.1.call-done = (f32[96,2592]{1,0:T(8,128)}, f32[96,2592]{1,0:T(8,128)}) async-done(((f32[96,2592]{1,0:T(8,128)}, f32[96,2592]{1,0:T(8,128)}), (f32[96,2592]{1,0:T(8,128)}, f32[96,2592]{1,0:T(8,128)})) %all-reduce.11.cloned.1.call-update) | async-done | bytes 1990672 | tf_op jit(solution)/shard_map/psum | solution.py:170
  (236 shorter events, 140.5 us)
Async XLA Ops:
  7.2 10.9 %copy-start.36 = (s32[2]{0:T(128)S(1)}, s32[2]{0:T(128)}, u32[]{:S(2)}) copy-start(s32[2]{0:T(128)} %param.25) | copy-start | bytes 28
  7.2 447.1 %all-reduce.11.cloned.1.call-start = ((), (), s32[]{:S(2)}) async-start(), calls=%async_computation | async-start | bytes 4128768 | tf_op jit(solution)/shard_map/psum | solution.py:170
  11.4 18.9 %copy-start.2 = (bf16[96,2592]{1,0:T(8,128)(2,1)S(1)}, bf16[96,2592]{1,0:T(8,128)(2,1)}, u32[]{:S(2)}) copy-start(bf16[96,2592]{1,0:T(8,128)(2,1)} %param.27) | copy-start | bytes 1492996
  11.8 6.5 %collective-permute-start = (bf16[96,1,16,8]{0,3,2,1:T(8,128)(2,1)S(1)}, bf16[96,1,16,8]{0,3,2,1:T(8,128)(2,1)S(1)}, u32[]{:S(2)}, u32[]{:S(2)}) collective-permute-start(bf16[96,1,16,8]{0,3,2,1:T(8,128)(2,1)S(1)} %get-tuple-element.576), channel_id=1, source_target_pairs={{0,4},{4,8},{8,12},{1,5},{5,9},{9,13},{2,6},{6,10},{10,14},{3,7},{... | collective-permute-start | bytes 73736 | tf_op jit(solution)/shard_map/ppermute | solution.py:16
  16.8 5.8 %collective-permute-start.1 = (bf16[96,1,16,8]{0,3,2,1:T(8,128)(2,1)S(1)}, bf16[96,1,16,8]{0,3,2,1:T(8,128)(2,1)S(1)}, u32[]{:S(2)}, u32[]{:S(2)}) collective-permute-start(bf16[96,1,16,8]{0,3,2,1:T(8,128)(2,1)S(1)} %get-tuple-element.577), channel_id=1, source_target_pairs={{4,0},{8,4},{12,8},{5,1},{9,5},{13,9},{6,2},{10,6},{14,10},{7,3},{... | collective-permute-start | bytes 73736 | tf_op jit(solution)/shard_map/ppermute | solution.py:17
  22.6 2.8 collective-permute-start.2
  23.9 4.8 %collective-permute-start.3 = (bf16[96,18,1,8]{0,3,2,1:T(8,128)(2,1)S(1)}, bf16[96,18,1,8]{0,3,2,1:T(8,128)(2,1)S(1)}, u32[]{:S(2)}, u32[]{:S(2)}) collective-permute-start(bf16[96,18,1,8]{0,3,2,1:T(8,128)(2,1)S(1)} %get-tuple-element.569), channel_id=1, source_target_pairs={{1,0},{2,1},{3,2},{5,4},{6,5},{7,6},{9,8},{10,9},{11,10},{13,12},{... | collective-permute-start | bytes 82952 | tf_op jit(solution)/shard_map/ppermute | solution.py:17
  30.3 60.2 %copy-start.15 = (f32[96]{0:T(128)S(1)}, f32[96]{0:T(128)}, u32[]{:S(2)}) copy-start(f32[96]{0:T(128)} %param.29) | copy-start | bytes 1156
  56.6 47.0 %copy-start.23 = (s32[2,3]{1,0:T(2,128)}, s32[2,3]{1,0:T(2,128)S(1)}, u32[]{:S(2)}) copy-start(s32[2,3]{1,0:T(2,128)S(1)} %get-tuple-element.1357) | copy-start | bytes 76
  56.6 42.5 %copy-start.3 = (bf16[96,2592]{1,0:T(8,128)(2,1)S(1)}, bf16[96,2592]{1,0:T(8,128)(2,1)}, u32[]{:S(2)}) copy-start(bf16[96,2592]{1,0:T(8,128)(2,1)} %param.28) | copy-start | bytes 1492996
  96.5 12.9 %copy-start.7 = (bf16[96,2,8,2,8,1,8]{0,6,5,4,3,2,1:T(8,128)(2,1)}, bf16[96,2,8,2,8,1,8]{0,6,5,4,3,2,1:T(8,128)(2,1)S(1)}, u32[]{:S(2)}) copy-start(bf16[96,2,8,2,8,1,8]{0,6,5,4,3,2,1:T(8,128)(2,1)S(1)} %copy.58) | copy-start | bytes 1179652
  96.5 3.7 collective-permute-start.4
  97.8 5.8 %collective-permute-start.5 = (bf16[96,1,16,8]{0,3,2,1:T(8,128)(2,1)S(1)}, bf16[96,1,16,8]{0,3,2,1:T(8,128)(2,1)S(1)}, u32[]{:S(2)}, u32[]{:S(2)}) collective-permute-start(bf16[96,1,16,8]{0,3,2,1:T(8,128)(2,1)S(1)} %get-tuple-element.575), channel_id=1, source_target_pairs={{4,0},{8,4},{12,8},{5,1},{9,5},{13,9},{6,2},{10,6},{14,10},{7,3},{... | collective-permute-start | bytes 73736 | tf_op jit(solution)/shard_map/ppermute | solution.py:17
  103.6 5.7 %collective-permute-start.6 = (bf16[96,18,1,8]{0,3,2,1:T(8,128)(2,1)S(1)}, bf16[96,18,1,8]{0,3,2,1:T(8,128)(2,1)S(1)}, u32[]{:S(2)}, u32[]{:S(2)}) collective-permute-start(bf16[96,18,1,8]{0,3,2,1:T(8,128)(2,1)S(1)} %get-tuple-element.566), channel_id=1, source_target_pairs={{0,1},{1,2},{2,3},{4,5},{5,6},{6,7},{8,9},{9,10},{10,11},{12,13},{... | collective-permute-start | bytes 82952 | tf_op jit(solution)/shard_map/ppermute | solution.py:16
  104.9 4.4 collective-permute-start.7
  111.9 58.9 %copy-start.17 = (f32[96]{0:T(128)S(1)}, f32[96]{0:T(128)}, u32[]{:S(2)}) copy-start(f32[96]{0:T(128)} %param.31) | copy-start | bytes 1156
  111.9 59.5 %copy-start.33 = (f32[96]{0:T(128)S(1)}, f32[96]{0:T(128)}, u32[]{:S(2)}) copy-start(f32[96]{0:T(128)} %param.32) | copy-start | bytes 1156
  111.9 94.7 %copy-start.37 = (s32[2]{0:T(128)S(1)}, s32[2]{0:T(128)}, u32[]{:S(2)}) copy-start(s32[2]{0:T(128)} %param.25) | copy-start | bytes 28
  140.0 74.7 %copy-start.8 = (bf16[96,2592]{0,1:T(8,128)(2,1)S(1)}, bf16[96,2592]{0,1:T(8,128)(2,1)}, u32[]{:S(2)}) copy-start(bf16[96,2592]{0,1:T(8,128)(2,1)} %copy.70) | copy-start | bytes 1492996
  203.4 12.2 %copy-start.34 = (f32[96]{0:T(128)}, f32[96]{0:T(128)S(1)}, u32[]{:S(2)}) copy-start(f32[96]{0:T(128)S(1)} %get-tuple-element.370) | copy-start | bytes 1156
  211.9 9.8 %collective-permute-start.8 = (bf16[96,1,16,8]{0,3,2,1:T(8,128)(2,1)S(1)}, bf16[96,1,16,8]{0,3,2,1:T(8,128)(2,1)S(1)}, u32[]{:S(2)}, u32[]{:S(2)}) collective-permute-start(bf16[96,1,16,8]{0,3,2,1:T(8,128)(2,1)S(1)} %get-tuple-element.572), channel_id=1, source_target_pairs={{0,4},{4,8},{8,12},{1,5},{5,9},{9,13},{2,6},{6,10},{10,14},{3,7},{... | collective-permute-start | bytes 73736 | tf_op jit(solution)/shard_map/ppermute | solution.py:16
  213.2 8.5 %collective-permute-start.9 = (bf16[96,1,16,8]{0,3,2,1:T(8,128)(2,1)S(1)}, bf16[96,1,16,8]{0,3,2,1:T(8,128)(2,1)S(1)}, u32[]{:S(2)}, u32[]{:S(2)}) collective-permute-start(bf16[96,1,16,8]{0,3,2,1:T(8,128)(2,1)S(1)} %get-tuple-element.573), channel_id=1, source_target_pairs={{4,0},{8,4},{12,8},{5,1},{9,5},{13,9},{6,2},{10,6},{14,10},{7,3},{... | collective-permute-start | bytes 73736 | tf_op jit(solution)/shard_map/ppermute | solution.py:17
  222.5 31.5 %collective-permute-start.10 = (bf16[96,18,1,8]{0,3,2,1:T(8,128)(2,1)S(1)}, bf16[96,18,1,8]{0,3,2,1:T(8,128)(2,1)}, u32[]{:S(2)}, u32[]{:S(2)}) collective-permute-start(bf16[96,18,1,8]{0,3,2,1:T(8,128)(2,1)S(1)} %get-tuple-element.564), channel_id=1, source_target_pairs={{0,1},{1,2},{2,3},{4,5},{5,6},{6,7},{8,9},{9,10},{10,11},{12,13},{... | collective-permute-start | bytes 82952 | tf_op jit(solution)/shard_map/ppermute | solution.py:16
  224.9 29.1 %collective-permute-start.11 = (bf16[96,18,1,8]{0,3,2,1:T(8,128)(2,1)S(1)}, bf16[96,18,1,8]{0,3,2,1:T(8,128)(2,1)}, u32[]{:S(2)}, u32[]{:S(2)}) collective-permute-start(bf16[96,18,1,8]{0,3,2,1:T(8,128)(2,1)S(1)} %get-tuple-element.565), channel_id=1, source_target_pairs={{1,0},{2,1},{3,2},{5,4},{6,5},{7,6},{9,8},{10,9},{11,10},{13,12},{... | collective-permute-start | bytes 82952 | tf_op jit(solution)/shard_map/ppermute | solution.py:17
  256.7 27.0 %copy-start.16 = (f32[96]{0:T(128)S(1)}, f32[96]{0:T(128)}, u32[]{:S(2)}) copy-start(f32[96]{0:T(128)} %param.30) | copy-start | bytes 1156
  256.7 63.0 %copy-start.18 = (f32[96]{0:T(128)S(1)}, f32[96]{0:T(128)}, u32[]{:S(2)}) copy-start(f32[96]{0:T(128)} %get-tuple-element.378) | copy-start | bytes 1156
  256.7 64.9 %copy-start.38 = (s32[2]{0:T(128)S(1)}, s32[2]{0:T(128)}, u32[]{:S(2)}) copy-start(s32[2]{0:T(128)} %param.25) | copy-start | bytes 28
  283.7 47.0 %copy-start = (f32[96,2592]{1,0:T(8,128)S(1)}, f32[96,2592]{1,0:T(8,128)}, u32[]{:S(2)}) copy-start(f32[96,2592]{1,0:T(8,128)} %custom-call) | copy-start | bytes 2985988
  327.5 29.4 %collective-permute-start.12 = (bf16[96,1,16,8]{0,3,2,1:T(8,128)(2,1)}, bf16[96,1,16,8]{0,3,2,1:T(8,128)(2,1)}, u32[]{:S(2)}, u32[]{:S(2)}) collective-permute-start(bf16[96,1,16,8]{0,3,2,1:T(8,128)(2,1)} %get-tuple-element.570), channel_id=1, source_target_pairs={{0,4},{4,8},{8,12},{1,5},{5,9},{9,13},{2,6},{6,10},{10,14},{3,7},{... | collective-permute-start | bytes 73736 | tf_op jit(solution)/shard_map/ppermute | solution.py:16
  329.4 27.5 %collective-permute-start.13 = (bf16[96,1,16,8]{0,3,2,1:T(8,128)(2,1)}, bf16[96,1,16,8]{0,3,2,1:T(8,128)(2,1)}, u32[]{:S(2)}, u32[]{:S(2)}) collective-permute-start(bf16[96,1,16,8]{0,3,2,1:T(8,128)(2,1)} %get-tuple-element.571), channel_id=1, source_target_pairs={{4,0},{8,4},{12,8},{5,1},{9,5},{13,9},{6,2},{10,6},{14,10},{7,3},{... | collective-permute-start | bytes 73736 | tf_op jit(solution)/shard_map/ppermute | solution.py:17
  357.7 3.4 collective-permute-start.14
  359.0 3.1 collective-permute-start.15
  (36 other events, 103.8 us)
Sparse Core Ops, SparseCore 0:
  357.0 97.2 all-reduce.10
where the time goes:
time: 472 us; the launch traced here: 464 us
  local copies, waits for them, and re-layouts  143 us (30%)
  blocking collectives  126 us (27%)
  waiting for transfers between devices  68.5 us (15%)
  matrix products  41 us (9%)
  other arithmetic  29 us (6%)
  starting transfers between devices  26.4 us (6%)
  loops' own time  16 us (3%)
  between operations  15.3 us (3%)
    concatenate x12, local copies, waits for them, and re-layouts, unfold(): return jnp.concatenate(pieces, axis=0)  70.8 us
    psum x2, blocking collectives, norm_forward(): lax.psum((jnp.sum(values, axis=(0, 2)), jnp.sum(values * values, axis=(0,...  63.4 us
    psum x2, blocking collectives, norm_back(): lax.psum((jnp.sum(grad_z, axis=(0, 2)), jnp.sum(grad_z * normed, axis=(0,...  62.4 us
    psum x1, waiting for transfers between devices, per_device(): total_one = lax.psum(partial_one, ('gx', 'gy'))  56.2 us
    slice x12, local copies, waits for them, and re-layouts, unfold(): window[:, step_x:step_x + 8, step_y:step_y + 8, step_z:step_z + 8]  33.6 us
    dot_general x8, matrix products, one_block(): jnp.dot(weight, block_window(padded, corner), preferred_element_type=jnp....  24 us
    ppermute x8, starting transfers between devices, extended(): before = lax.ppermute(last, axis, up)  15.6 us
    dot_general x4, matrix products, add_block(): lax.dot_general(piece, columns, (((1,), (1,)), ((), ())), preferred_eleme...  12.2 us
  transfers between devices with their start and end apart: 17, of which 6 were waited for; matrix products, arithmetic and copies ran while one was open for 20% of the time, Pallas kernels for 0%

commit v1 on v0

v1 whole, which is shorter than its diff:
```python
import functools

import jax
import jax.numpy as jnp
from jax import lax
from jax.experimental import pallas as pl
from jax.experimental.pallas import tpu as pltpu
from jax.sharding import PartitionSpec as P

EPS = 1e-05
F32, BF16 = jnp.float32, jnp.bfloat16
MESH = pl.DeviceIdType.MESH
C = 96
PLANES = 16
SIDES = ((1, 0), (-1, 0), (0, 1), (0, -1), (1, 1), (1, -1), (-1, 1), (-1, -1))
COLS = 27 * C
GROWS = 2048


def silu_slope(values):
    sigma = jax.nn.sigmoid(values)
    return sigma * (1.0 + values * (1.0 - sigma))


def lanes(rows=C):
    return lax.broadcasted_iota(jnp.int32, (rows, 128), 1)


def roll(tile, shift):
    return pltpu.roll(tile, shift, 1)


def kernel(nx, ny, slot_ref, count_ref, mask_ref, params_ref, feats_ref, cot_ref, w1_ref, w2_ref,
           f1_ref, f2_ref,
           out_ref, fg_ref, wg1_ref, wg2_ref, ng_ref,
           rmask, field, cot, val1, val2, tmp, flat, xa, xb, xc, halo, packs, stat_src, stats,
           grad, parts, share, full,
           halo_send, halo_recv, stat_send, stat_recv, rs_send, rs_recv, ag_send, ag_recv):
    group = nx * ny
    gx, gy = lax.axis_index("gx"), lax.axis_index("gy")
    me = gx * ny + gy
    chunk = GROWS // group

    def ident(peer):
        return {"gx": peer // ny, "gy": lax.rem(peer, ny)}

    def each_peer(body):
        def step(j, carry):
            body(j, lax.rem(me + j, group))
            return carry
        lax.fori_loop(1, group, step, 0)

    barrier = pltpu.get_barrier_semaphore()
    each_peer(lambda j, peer: pl.semaphore_signal(
        barrier, inc=1, device_id=ident(peer), device_id_type=MESH))

    live = [(k < count_ref[0]).astype(F32) for k in range(2)]
    hot = [[(slot_ref[k] == s).astype(F32) for s in range(4)] for k in range(2)]

    def place(tile_of, rows, store):
        low = lanes(rows) < 64
        for t in range(4):
            tiles = [tile_of(k, t) for k in range(2)]
            turned = [roll(x, 64) for x in tiles]
            for sx in range(2):
                first = sum(jnp.where(low, hot[k][2 * sx] * tiles[k], hot[k][2 * sx + 1] * turned[k])
                            for k in range(2))
                second = sum(jnp.where(low, hot[k][2 * sx] * turned[k], hot[k][2 * sx + 1] * tiles[k])
                             for k in range(2))
                store(sx * 8 + 2 * t, first)
                store(sx * 8 + 2 * t + 1, second)

    def take(src, ref):
        low = lanes() < 64
        for t in range(4):
            acc = [jnp.zeros((C, 128), F32) for _ in range(2)]
            for sx in range(2):
                a, b = src[sx * 8 + 2 * t], src[sx * 8 + 2 * t + 1]
                left = jnp.where(low, a, roll(b, 64))
                right = jnp.where(low, roll(a, 64), b)
                for k in range(2):
                    acc[k] = acc[k] + hot[k][2 * sx] * left + hot[k][2 * sx + 1] * right
            for k in range(2):
                ref[k, :, t * 128:(t + 1) * 128] = acc[k].astype(BF16)

    def store_mask(p, value):
        rmask[p] = value

    def store_input(p, value):
        field[0, p] = (value * rmask[p][0:1]).astype(BF16)

    def store_cot(p, value):
        cot[p] = (value * rmask[p][0:1]).astype(BF16)

    place(lambda k, t: jnp.broadcast_to(
        mask_ref[k:k + 1, t * 128:(t + 1) * 128].astype(F32) * live[k], (8, 128)), 8, store_mask)
    place(lambda k, t: feats_ref[k, :, t * 128:(t + 1) * 128].astype(F32), C, store_input)

    def halo_copy(ex, d, src):
        dx, dy = SIDES[d]
        return pltpu.make_async_remote_copy(
            src_ref=src, dst_ref=halo.at[ex, d],
            send_sem=halo_send.at[ex, d], recv_sem=halo_recv.at[ex, d],
            device_id={"gx": gx + dx, "gy": gy + dy}, device_id_type=MESH)

    def inside(dx, dy):
        return (gx + dx >= 0) & (gx + dx < nx) & (gy + dy >= 0) & (gy + dy < ny)

    def halo_sources(ex):
        srcs = []
        for d, (dx, dy) in enumerate(SIDES):
            if dx == 0:
                srcs.append(packs.at[ex, 0 if dy == 1 else 1])
            else:
                srcs.append(field.at[ex, PLANES - 1 if dx == 1 else 0])
        return srcs

    for d, (dx, dy) in enumerate(SIDES):
        @pl.when(jnp.logical_not(inside(-dx, -dy)))
        def _(d=d):
            for ex in range(4):
                halo[ex, d] = jnp.zeros((C, 128), BF16)

    def send_halo(ex):
        lane = lanes()

        def pack(i, carry):
            high, low = carry
            plane = field[ex, i].astype(F32)
            here = (lane >= i * 8) & (lane < i * 8 + 8)
            high = jnp.where(here, roll(plane, lax.rem(i * 8 + 8, 128)), high)
            low = jnp.where(here, roll(plane, i * 8), low)
            return high, low

        zero = jnp.zeros((C, 128), F32)
        high, low = lax.fori_loop(0, PLANES, pack, (zero, zero))
        packs[ex, 0] = high.astype(BF16)
        packs[ex, 1] = low.astype(BF16)
        srcs = halo_sources(ex)
        for d, (dx, dy) in enumerate(SIDES):
            @pl.when(inside(dx, dy))
            def _(d=d):
                halo_copy(ex, d, srcs[d]).start()

    def wait_halo(ex):
        srcs = halo_sources(ex)
        for d, (dx, dy) in enumerate(SIDES):
            @pl.when(inside(-dx, -dy))
            def _(d=d):
                halo_copy(ex, d, srcs[d]).wait_recv()

    def done_halo(ex):
        srcs = halo_sources(ex)
        for d, (dx, dy) in enumerate(SIDES):
            @pl.when(inside(dx, dy))
            def _(d=d):
                halo_copy(ex, d, srcs[d]).wait_send()

    def side(ex, dx, dy):
        return halo[ex, SIDES.index((-dx, -dy))].astype(F32)

    def spread(x, p, plane, edge):
        lane = lanes()
        z = lane % 8
        for oy in (-1, 0, 1):
            src = plane
            if oy == 1:
                src = jnp.where(lane < 8, edge, plane)
            elif oy == -1:
                src = jnp.where(lane >= 120, edge, plane)
            for oz in (-1, 0, 1):
                shift = (-(8 * oy + oz)) % 128
                r = roll(src, shift) if shift else src
                if oz == 1:
                    r = jnp.where(z < 7, r, 0.0)
                elif oz == -1:
                    r = jnp.where(z > 0, r, 0.0)
                row = ((oy + 1) * 3 + oz + 1) * C
                start = p * 128 if isinstance(p, int) else pl.multiple_of(p * 128, 128)
                x[row:row + C, pl.ds(start, 128)] = r.astype(BF16)

    def unfold(ex, x):
        lane = lanes()
        for p, dx in ((0, -1), (PLANES + 1, 1)):
            edge = jnp.where(lane < 64, side(ex, dx, 1), side(ex, dx, -1))
            spread(x, p, side(ex, dx, 0), edge)

        def body(i, carry):
            before = roll(side(ex, 0, -1), lax.rem(248 - i * 8, 128))
            after = roll(side(ex, 0, 1), lax.rem(128 - i * 8, 128))
            spread(x, i + 1, field[ex, i].astype(F32), jnp.where(lane < 64, after, before))
            return carry
        lax.fori_loop(0, PLANES, body, 0)

    def conv(w_ref, x, store):
        def body(j, carry):
            acc = None
            for ox in range(3):
                cols = x[:, pl.ds(pl.multiple_of((2 * j + ox) * 128, 128), 256)]
                part = jnp.dot(w_ref[ox], cols, preferred_element_type=F32)
                acc = part if acc is None else acc + part
            for h in range(2):
                carry = store(2 * j + h, acc[:, h * 128:(h + 1) * 128], carry)
            return carry
        return body

    def run_conv(w_ref, x, store, init):
        return lax.fori_loop(0, PLANES // 2, conv(w_ref, x, store), init)

    def pack_columns(columns):
        lane = lanes(C)
        tile = jnp.zeros((C, 128), F32)
        for i, column in enumerate(columns):
            tile = jnp.where(lane == i, column, tile)
        whole = jnp.concatenate([tile, jnp.zeros((128 - C, 128), F32)], axis=0)
        return jnp.transpose(whole)[0:8]

    def to_columns(rows):
        whole = jnp.concatenate(rows + [jnp.zeros((128 - len(rows), 128), F32)], axis=0)
        turned = jnp.transpose(whole)
        return [turned[0:C, i:i + 1] for i in range(len(rows))]

    def stat_copy(ph, j, peer, slot):
        return pltpu.make_async_remote_copy(
            src_ref=stat_src.at[ph], dst_ref=stats.at[ph, slot],
            send_sem=stat_send.at[ph, j], recv_sem=stat_recv.at[ph, slot],
            device_id=ident(peer), device_id_type=MESH)

    def send_stats(ph, tile):
        stat_src[ph] = tile
        stats[ph, me] = tile
        each_peer(lambda j, peer: stat_copy(ph, j, peer, me).start())

    def wait_stats(ph):
        each_peer(lambda j, peer: stat_copy(ph, j, peer, peer).wait_recv())

    def done_stats(ph):
        each_peer(lambda j, peer: stat_copy(ph, j, peer, me).wait_send())

    def total_stats(ph):
        return lax.fori_loop(0, group, lambda i, acc: acc + stats[ph, i], jnp.zeros((8, 128), F32))

    def total(tile):
        return jnp.sum(tile, axis=1, keepdims=True)

    zero_tile = jnp.zeros((C, 128), F32)
    here = lax.fori_loop(0, PLANES, lambda i, acc: acc + rmask[i], jnp.zeros((8, 128), F32))
    here = jnp.sum(here[0:1], axis=1, keepdims=True)

    def moments(ph, val, summed):
        mean = total(summed) / jnp.maximum(here, 1.0)

        def body(i, acc):
            centred = (val[i] - mean) * rmask[i][0:1]
            return acc + centred * centred
        spread_sum = total(lax.fori_loop(0, PLANES, body, zero_tile))
        send_stats(ph, pack_columns([total(summed), spread_sum, jnp.broadcast_to(here, (C, 1))]))
        wait_stats(ph)
        sums = total_stats(ph)
        count = jnp.maximum(jnp.max(sums[2:3], axis=1, keepdims=True), 1.0)
        mean_row = sums[0:1] / count

        def shifted(i, acc):
            tile = stats[ph, i]
            n = tile[2:3]
            gap = tile[0:1] / jnp.maximum(n, 1.0) - mean_row
            return acc + tile[1:2] + n * gap * gap
        square = lax.fori_loop(0, group, shifted, jnp.zeros((1, 128), F32))
        inv_row = lax.rsqrt(square / count + EPS)
        mean_col, inv_col = to_columns([mean_row, inv_row])
        return mean_col, inv_col, 1.0 / count

    def store_conv(val):
        def store(p, tile, acc):
            y = tile * rmask[p][0:1]
            val[p] = y
            return acc + y
        return store

    gain1, shift1, gain2, shift2 = to_columns([params_ref[i:i + 1] for i in range(4)])

    pl.semaphore_wait(barrier, group - 1)
    send_halo(0)
    place(lambda k, t: cot_ref[k, :, t * 128:(t + 1) * 128].astype(F32), C, store_cot)
    wait_halo(0)
    unfold(0, xa)
    summed = run_conv(w1_ref, xa, store_conv(val1), zero_tile)
    mean1, inv1, per = moments(0, val1, summed)

    def act_one(i, carry):
        m = rmask[i][0:1]
        normed = (val1[i] - mean1) * m * inv1
        val1[i] = normed
        z = normed * gain1 + shift1
        field[1, i] = (z * jax.nn.sigmoid(z) * m).astype(BF16)
        return carry
    lax.fori_loop(0, PLANES, act_one, 0)

    send_halo(1)
    wait_halo(1)
    unfold(1, xb)
    summed = run_conv(w2_ref, xb, store_conv(val2), zero_tile)
    mean2, inv2, per = moments(1, val2, summed)

    def act_two(i, carry):
        a, b = carry
        m = rmask[i][0:1]
        normed = (val2[i] - mean2) * m * inv2
        val2[i] = normed
        z = normed * gain2 + shift2
        sigma = jax.nn.sigmoid(z)
        tmp[0, i] = z * sigma * m
        gz = cot[i].astype(F32) * (sigma * (1.0 + z * (1.0 - sigma)))
        tmp[1, i] = gz
        return a + gz, b + gz * normed
    sg, gg = lax.fori_loop(0, PLANES, act_two, (zero_tile, zero_tile))

    def send_back(ph, sg, gg):
        send_stats(ph, pack_columns([total(sg), total(gg)]))

    def finish_back(ph, row):
        wait_stats(ph)
        sums = total_stats(ph)
        ng_ref[row:row + 1, :] = sums[1:2, 0:C]
        ng_ref[row + 1:row + 2, :] = sums[0:1, 0:C]
        return to_columns([sums[0:1], sums[1:2]])

    def back(ex, val, gz_slot, gain, inv, sums):
        sg, gg = sums[0] * per, sums[1] * per
        scaled = gain * inv

        def body(i, carry):
            g = rmask[i][0:1] * scaled * (tmp[gz_slot, i] - sg - val[i] * gg)
            g = g.astype(BF16)
            field[ex, i] = g
            flat[:, pl.ds(pl.multiple_of(i * 128, 128), 128)] = g
            return carry
        lax.fori_loop(0, PLANES, body, 0)

    send_back(2, sg, gg)
    take(tmp.at[0], out_ref)
    back(2, val2, 1, gain2, inv2, finish_back(2, 2))
    send_halo(2)

    def kernel_grad(w, x):
        for b in range((COLS + 255) // 256):
            lo, hi = b * 256, min(b * 256 + 256, COLS)
            pieces = []
            for ox in range(3):
                first, last = max(lo, ox * 9 * C), min(hi, (ox + 1) * 9 * C)
                if first < last:
                    pieces.append(x[first - ox * 9 * C:last - ox * 9 * C,
                                    ox * 128:ox * 128 + PLANES * 128])
            rhs = pieces[0] if len(pieces) == 1 else jnp.concatenate(pieces, axis=0)
            part = lax.dot_general(flat[...], rhs, (((1,), (1,)), ((), ())),
                                   preferred_element_type=F32).astype(BF16)
            for h in range(0, hi - lo, 128):
                tile = part[:, h:min(h + 128, hi - lo)]
                if tile.shape[1] < 128:
                    tile = jnp.concatenate(
                        [tile, jnp.zeros((C, 128 - tile.shape[1]), BF16)], axis=1)
                row = (lo + h) // 128 * C
                grad[w, row:row + C] = tile
        grad[w, 21 * C:GROWS] = jnp.zeros((GROWS - 21 * C, 128), BF16)

    def rows_of(i):
        return pl.ds(pl.multiple_of(i * chunk, chunk), chunk)

    def rs_copy(w, j, peer, slot):
        return pltpu.make_async_remote_copy(
            src_ref=grad.at[w, rows_of(peer)], dst_ref=parts.at[w, slot],
            send_sem=rs_send.at[w, j], recv_sem=rs_recv.at[w, slot],
            device_id=ident(peer), device_id_type=MESH)

    def ag_copy(w, j, peer, slot):
        return pltpu.make_async_remote_copy(
            src_ref=share.at[w], dst_ref=full.at[w, rows_of(slot)],
            send_sem=ag_send.at[w, j], recv_sem=ag_recv.at[w, slot],
            device_id=ident(peer), device_id_type=MESH)

    def start_rs(w):
        parts[w, me] = grad[w, rows_of(me)]
        each_peer(lambda j, peer: rs_copy(w, j, peer, me).start())

    def finish_rs(w):
        each_peer(lambda j, peer: rs_copy(w, j, peer, peer).wait_recv())
        summed = lax.fori_loop(0, group, lambda i, acc: acc + parts[w, i].astype(F32),
                               jnp.zeros((chunk, 128), F32)).astype(BF16)
        share[w] = summed
        full[w, rows_of(me)] = summed
        each_peer(lambda j, peer: ag_copy(w, j, peer, me).start())

    def finish_ag(w, ref):
        each_peer(lambda j, peer: ag_copy(w, j, peer, peer).wait_recv())
        for t in range(21):
            wide = min(128, COLS - t * 128)
            ref[:, t * 128:t * 128 + wide] = full[w, t * C:(t + 1) * C].astype(F32)[:, 0:wide]

    kernel_grad(1, xb)
    start_rs(1)
    wait_halo(2)
    unfold(2, xc)

    def store_gz(p, tile, carry):
        a, b = carry
        normed = val1[p]
        z = normed * gain1 + shift1
        gz = tile * rmask[p][0:1] * silu_slope(z)
        tmp[0, p] = gz
        return a + gz, b + gz * normed
    sg, gg = run_conv(f2_ref, xc, store_gz, (zero_tile, zero_tile))
    send_back(3, sg, gg)
    finish_rs(1)
    back(3, val1, 0, gain1, inv1, finish_back(3, 0))
    send_halo(3)
    kernel_grad(0, xa)
    start_rs(0)
    wait_halo(3)
    unfold(3, xc)

    def store_fg(p, tile, carry):
        tmp[1, p] = tile * rmask[p][0:1]
        return carry
    run_conv(f1_ref, xc, store_fg, 0)
    take(tmp.at[1], fg_ref)
    finish_rs(0)
    finish_ag(1, wg2_ref)
    finish_ag(0, wg1_ref)

    for ex in range(4):
        done_halo(ex)
        done_stats(ex)
    for w in range(2):
        each_peer(lambda j, peer: rs_copy(w, j, peer, me).wait_send())
        each_peer(lambda j, peer: ag_copy(w, j, peer, me).wait_send())


def split(weight):
    return weight.reshape(C, 3, 9 * C).transpose(1, 0, 2)


def flipped(weight):
    return jnp.flip(weight.reshape(C, 3, 9, C), axis=(1, 2)).transpose(1, 3, 2, 0).reshape(3, C, 9 * C)


def per_device(nx, ny, feats, voxel_mask, block_slot, block_count, weight_one, weight_two,
               gain_one, shift_one, gain_two, shift_two, cotangent):
    group = nx * ny
    params = jnp.pad(jnp.stack([gain_one, shift_one, gain_two, shift_two]), ((0, 4), (0, 128 - C)))
    vmem = pl.BlockSpec(memory_space=pltpu.VMEM)
    smem = pl.BlockSpec(memory_space=pltpu.SMEM)
    shapes = [
        jax.ShapeDtypeStruct((2, C, 512), BF16),
        jax.ShapeDtypeStruct((2, C, 512), BF16),
        jax.ShapeDtypeStruct((C, COLS), F32),
        jax.ShapeDtypeStruct((C, COLS), F32),
        jax.ShapeDtypeStruct((4, C), F32),
    ]
    wide = (PLANES + 2) * 128
    dma = pltpu.SemaphoreType.DMA
    return pl.pallas_call(
        functools.partial(kernel, nx, ny),
        out_shape=shapes,
        in_specs=[smem, smem] + [vmem] * 8,
        out_specs=[vmem] * 5,
        scratch_shapes=[
            pltpu.VMEM((PLANES, 8, 128), F32),
            pltpu.VMEM((4, PLANES, C, 128), BF16),
            pltpu.VMEM((PLANES, C, 128), BF16),
            pltpu.VMEM((PLANES, C, 128), F32),
            pltpu.VMEM((PLANES, C, 128), F32),
            pltpu.VMEM((2, PLANES, C, 128), F32),
            pltpu.VMEM((C, PLANES * 128), BF16),
            pltpu.VMEM((9 * C, wide), BF16),
            pltpu.VMEM((9 * C, wide), BF16),
            pltpu.VMEM((9 * C, wide), BF16),
            pltpu.VMEM((4, 8, C, 128), BF16),
            pltpu.VMEM((4, 2, C, 128), BF16),
            pltpu.VMEM((4, 8, 128), F32),
            pltpu.VMEM((4, group, 8, 128), F32),
            pltpu.VMEM((2, GROWS, 128), BF16),
            pltpu.VMEM((2, group, GROWS // group, 128), BF16),
            pltpu.VMEM((2, GROWS // group, 128), BF16),
            pltpu.VMEM((2, GROWS, 128), BF16),
            dma((4, 8)), dma((4, 8)),
            dma((4, group)), dma((4, group)),
            dma((2, group)), dma((2, group)),
            dma((2, group)), dma((2, group)),
        ],
        compiler_params=pltpu.CompilerParams(
            collective_id=0, has_side_effects=True, vmem_limit_bytes=48 * 1024 * 1024),
        name="section",
    )(block_slot, block_count, voxel_mask, params, feats, cotangent,
      split(weight_one), split(weight_two), flipped(weight_one), flipped(weight_two))


def solution(mesh):
    rows = ("scene", "gx", "gy")
    placed = (
        P(rows, None, None), P(rows, None), P(rows), P(rows),
        P(), P(), P(), P(), P(), P(), P(rows, None, None),
    )
    return jax.shard_map(
        functools.partial(per_device, mesh.shape["gx"], mesh.shape["gy"]),
        mesh=mesh,
        in_specs=placed,
        out_specs=(
            P(rows, None, None), P(rows, None, None),
            P("scene", None), P("scene", None), P("scene", None),
        ),
        check_vma=False,
    )
```

time: 472 us -> 122 us (0.26)
  the two profiles are of different devices: /device:TPU:0 before, /device:TPU:11 now
where the time goes in v1:
time: 122 us
  Pallas kernels  109 us (89%)
  local copies, waits for them, and re-layouts  10.8 us (9%)
  between operations  1.43 us (1%)
    pallas_call x1, Pallas kernels, per_device(): pl.pallas_call(functools.partial(kernel, nx, ny), out_shape=shapes, in_sp...  109 us
    unnamed x27, local copies, waits for them, and re-layouts  8.51 us

profile of v1, /device:TPU:11, one launch (start us, length us, event | category | flops | bytes accessed | tf_op | source)
XLA Modules:
  0.0 121.7 jit_solution(2655376654049223615)
XLA Ops:
  1.3 0.0 copy-start.9
  1.3 0.0 copy-start.6
  1.3 0.6 copy-done.9
  1.9 0.0 copy-done.6
  2.0 0.0 copy-done.7
  2.0 0.0 copy-done.8
  2.0 1.4 %copy.20 = bf16[96,2592]{0,1:T(8,128)(2,1)S(1)} copy(bf16[96,2592]{1,0:T(8,128)(2,1)} %param.15) | data formatting | bytes 995328 | tf_op args[4]
  3.4 0.3 copy.21
  3.8 0.0 copy-start.5
  3.8 0.3 copy.24.f1_ref
  4.1 0.7 copy-done.5
  4.8 0.3 copy.22
  5.2 0.3 copy.23
  5.5 0.0 copy-start.4
  5.5 0.3 copy.25.f2_ref
  5.8 0.7 copy-done.4
  6.5 0.4 reshape.28
  7.0 0.4 reshape.29
  7.4 0.0 copy-start
  7.4 0.0 copy-start.1
  7.4 0.0 copy-start.2
  7.4 0.1 copy_bitcast_fusion
  7.5 0.0 copy-start.3
  7.5 0.8 copy-done
  8.3 0.1 copy-done.1
  8.4 0.0 copy-done.3
  8.4 109.4 %section.1 = (bf16[2,96,512]{2,1,0:T(8,128)(2,1)S(1)}, bf16[2,96,512]{2,1,0:T(8,128)(2,1)S(1)}, f32[96,2592]{1,0:T(8,128)S(1)}, f32[96,2592]{1,0:T(8,128)S(1)}, f32[4,96]{1,0:T(4,128)S(1)}) custom-call(s32[2]{0:T(128)S(1)} %copy-done.3, s32[1]{0:T(128)S(6)} %copy.33.count_ref, s32[2,512]{1,0:T(2,128)S(1)} %copy-done.2, ...), custom_call_target="tpu_custom_call" | custom-call | tf_op jit(solution)/shard_map/section/pallas_call | solution.py:461
  117.8 0.7 copy.34
  118.5 0.7 copy.35
  119.2 1.0 copy.36
  120.1 1.0 copy.37
  121.1 0.6 copy.38
  (6 shorter events, 0.1 us)
Async XLA Ops:
  1.3 0.7 copy-start.9
  1.3 0.7 copy-start.6
  1.3 0.7 copy-start.7
  1.3 0.7 copy-start.8
  3.8 1.0 copy-start.5
  5.5 1.0 copy-start.4
  7.4 0.9 copy-start
  7.4 1.0 copy-start.1
  7.4 1.0 copy-start.2
  7.5 0.9 copy-start.3

commit v2 on v1

--- a/solution.py
+++ b/solution.py
@@ -31,9 +31,8 @@
 
 
 def kernel(nx, ny, slot_ref, count_ref, mask_ref, params_ref, feats_ref, cot_ref, w1_ref, w2_ref,
-           f1_ref, f2_ref,
            out_ref, fg_ref, wg1_ref, wg2_ref, ng_ref,
-           rmask, field, cot, val1, val2, tmp, flat, xa, xb, xc, halo, packs, stat_src, stats,
+           rmask, field, cot, val1, val2, tmp, flat, xa, xb, xc, turned_w, f1_ref, f2_ref, halo, packs, stat_src, stats,
            grad, parts, share, full,
            halo_send, halo_recv, stat_send, stat_recv, rs_send, rs_recv, ag_send, ag_recv):
     group = nx * ny
@@ -192,12 +191,46 @@
             return carry
         lax.fori_loop(0, PLANES, body, 0)
 
+    def slabs():
+        return [(lo, min(lo + 256, COLS)) for lo in range(0, COLS, 256)]
+
+    def pieces_of(lo, hi):
+        found = []
+        for ox in range(3):
+            first, last = max(lo, ox * 9 * C), min(hi, (ox + 1) * 9 * C)
+            if first < last:
+                found.append((ox, first - ox * 9 * C, last - ox * 9 * C))
+        return found
+
+    def joined(pieces):
+        return pieces[0] if len(pieces) == 1 else jnp.concatenate(pieces, axis=0)
+
+    def flip(w_ref, out):
+        for lo in range(0, COLS, 128):
+            wide = min(128, COLS - lo)
+            tile = w_ref[:, lo:lo + wide].astype(F32)
+            if wide < 128:
+                tile = jnp.concatenate([tile, jnp.zeros((C, 128 - wide), F32)], axis=1)
+            tile = jnp.concatenate([tile, jnp.zeros((128 - C, 128), F32)], axis=0)
+            turned_w[lo:lo + 128] = jnp.transpose(tile)
+        lane = lanes()
+        for lo in range(0, COLS, 128):
+            tile = jnp.zeros((C, 128), F32)
+            for o in range(27):
+                to = o * C - lo
+                if to < 128 and to + C > 0:
+                    block = turned_w[(26 - o) * C:(27 - o) * C]
+                    block = roll(block, to % 128) if to % 128 else block
+                    tile = jnp.where((lane >= to) & (lane < to + C), block, tile)
+            out[:, lo:lo + 128] = tile.astype(BF16)
+
     def conv(w_ref, x, store):
         def body(j, carry):
             acc = None
-            for ox in range(3):
-                cols = x[:, pl.ds(pl.multiple_of((2 * j + ox) * 128, 128), 256)]
-                part = jnp.dot(w_ref[ox], cols, preferred_element_type=F32)
+            for lo, hi in slabs():
+                cols = [x[a:b, pl.ds(pl.multiple_of((2 * j + ox) * 128, 128), 256)]
+                        for ox, a, b in pieces_of(lo, hi)]
+                part = jnp.dot(w_ref[:, lo:hi], joined(cols), preferred_element_type=F32)
                 acc = part if acc is None else acc + part
             for h in range(2):
                 carry = store(2 * j + h, acc[:, h * 128:(h + 1) * 128], carry)
@@ -282,6 +315,8 @@
     pl.semaphore_wait(barrier, group - 1)
     send_halo(0)
     place(lambda k, t: cot_ref[k, :, t * 128:(t + 1) * 128].astype(F32), C, store_cot)
+    flip(w2_ref, f2_ref)
+    flip(w1_ref, f1_ref)
     wait_halo(0)
     unfold(0, xa)
     summed = run_conv(w1_ref, xa, store_conv(val1), zero_tile)
@@ -343,15 +378,9 @@
     send_halo(2)
 
     def kernel_grad(w, x):
-        for b in range((COLS + 255) // 256):
-            lo, hi = b * 256, min(b * 256 + 256, COLS)
-            pieces = []
-            for ox in range(3):
-                first, last = max(lo, ox * 9 * C), min(hi, (ox + 1) * 9 * C)
-                if first < last:
-                    pieces.append(x[first - ox * 9 * C:last - ox * 9 * C,
-                                    ox * 128:ox * 128 + PLANES * 128])
-            rhs = pieces[0] if len(pieces) == 1 else jnp.concatenate(pieces, axis=0)
+        for lo, hi in slabs():
+            rhs = joined([x[a:b, ox * 128:ox * 128 + PLANES * 128]
+                          for ox, a, b in pieces_of(lo, hi)])
             part = lax.dot_general(flat[...], rhs, (((1,), (1,)), ((), ())),
                                    preferred_element_type=F32).astype(BF16)
             for h in range(0, hi - lo, 128):
@@ -423,8 +452,8 @@
         return carry
     run_conv(f1_ref, xc, store_fg, 0)
     take(tmp.at[1], fg_ref)
+    finish_ag(1, wg2_ref)
     finish_rs(0)
-    finish_ag(1, wg2_ref)
     finish_ag(0, wg1_ref)
 
     for ex in range(4):
@@ -433,14 +462,6 @@
     for w in range(2):
         each_peer(lambda j, peer: rs_copy(w, j, peer, me).wait_send())
         each_peer(lambda j, peer: ag_copy(w, j, peer, me).wait_send())
-
-
-def split(weight):
-    return weight.reshape(C, 3, 9 * C).transpose(1, 0, 2)
-
-
-def flipped(weight):
-    return jnp.flip(weight.reshape(C, 3, 9, C), axis=(1, 2)).transpose(1, 3, 2, 0).reshape(3, C, 9 * C)
 
 
 def per_device(nx, ny, feats, voxel_mask, block_slot, block_count, weight_one, weight_two,
@@ -461,7 +482,7 @@
     return pl.pallas_call(
         functools.partial(kernel, nx, ny),
         out_shape=shapes,
-        in_specs=[smem, smem] + [vmem] * 8,
+        in_specs=[smem, smem] + [vmem] * 6,
         out_specs=[vmem] * 5,
         scratch_shapes=[
             pltpu.VMEM((PLANES, 8, 128), F32),
@@ -474,6 +495,9 @@
             pltpu.VMEM((9 * C, wide), BF16),
             pltpu.VMEM((9 * C, wide), BF16),
             pltpu.VMEM((9 * C, wide), BF16),
+            pltpu.VMEM((21 * 128, 128), F32),
+            pltpu.VMEM((C, 21 * 128), BF16),
+            pltpu.VMEM((C, 21 * 128), BF16),
             pltpu.VMEM((4, 8, C, 128), BF16),
             pltpu.VMEM((4, 2, C, 128), BF16),
             pltpu.VMEM((4, 8, 128), F32),
@@ -491,7 +515,7 @@
             collective_id=0, has_side_effects=True, vmem_limit_bytes=48 * 1024 * 1024),
         name="section",
     )(block_slot, block_count, voxel_mask, params, feats, cotangent,
-      split(weight_one), split(weight_two), flipped(weight_one), flipped(weight_two))
+      weight_one, weight_two)
 
 
 def solution(mesh):

time: 122 us -> 120 us (0.984)
  local copies, waits for them, and re-layouts: 10.8 us -> 9.09 us
    reshape x4 -> x0, local copies, waits for them, and re-layouts: 1.46 us -> none  [the longest x2 0.81 us: split(): return weight.reshape(C, 3, 9 * C).transpose(1, 0, 2)]
    unnamed x27 -> x25, local copies, waits for them, and re-layouts: 8.51 us -> 9.09 us
where the time goes in v2:
time: 120 us
  Pallas kernels  110 us (92%)
  local copies, waits for them, and re-layouts  9.09 us (8%)
  between operations  1.34 us (1%)
    pallas_call x1, Pallas kernels, per_device(): pl.pallas_call(functools.partial(kernel, nx, ny), out_shape=shapes, in_sp...  110 us
    unnamed x25, local copies, waits for them, and re-layouts  9.09 us

profile of v2, /device:TPU:11, one launch (start us, length us, event | category | flops | bytes accessed | tf_op | source)
XLA Modules:
  0.0 119.9 jit_solution(6609923168424568660)
XLA Ops:
  1.3 0.0 copy-start.6
  1.3 0.0 copy-start.7
  1.3 0.0 copy-start.8
  1.3 0.0 copy-start.9
  1.3 0.0 copy-start.4
  1.3 0.6 copy-done.6
  1.9 0.0 copy-done.7
  2.0 0.0 copy-done.8
  2.0 0.0 copy-done.9
  2.0 0.0 copy-start.5
  2.0 0.0 copy-done.4
  2.0 0.6 copy-done.5
  2.6 0.0 copy-start
  2.6 1.0 copy-done
  3.7 0.0 copy-start.1
  3.7 1.0 copy-done.1
  4.7 0.0 copy-start.2
  4.7 0.9 copy-done.2
  5.6 0.0 copy-start.3
  5.6 0.9 copy-done.3
  6.6 109.5 %section.1 = (bf16[2,96,512]{2,1,0:T(8,128)(2,1)S(1)}, bf16[2,96,512]{2,1,0:T(8,128)(2,1)S(1)}, f32[96,2592]{1,0:T(8,128)S(1)}, f32[96,2592]{1,0:T(8,128)S(1)}, f32[4,96]{1,0:T(4,128)S(1)}) custom-call(s32[2]{0:T(128)S(1)} %copy-done.5, s32[1]{0:T(128)S(6)} %copy.21.count_ref, s32[2,512]{1,0:T(2,128)S(1)} %copy-done.4, ...), custom_call_target="tpu_custom_call" | custom-call | tf_op jit(solution)/shard_map/section/pallas_call | solution.py:482
  116.1 0.7 copy.22
  116.8 0.7 copy.23
  117.4 1.0 copy.24
  118.4 1.0 copy.25
  119.4 0.6 copy.26
  (1 shorter events, 0.0 us)
Async XLA Ops:
  1.3 0.7 copy-start.6
  1.3 0.7 copy-start.7
  1.3 0.7 copy-start.8
  1.3 0.7 copy-start.9
  1.3 0.7 copy-start.4
  2.0 0.7 copy-start.5
  2.6 1.0 copy-start
  3.7 1.0 copy-start.1
  4.7 0.9 copy-start.2
  5.6 0.9 copy-start.3

commit v3 on v2

--- a/solution.py
+++ b/solution.py
@@ -14,6 +14,7 @@
 PLANES = 16
 SIDES = ((1, 0), (-1, 0), (0, 1), (0, -1), (1, 1), (1, -1), (-1, 1), (-1, -1))
 COLS = 27 * C
+TALL = C + 8
 GROWS = 2048
 
 
@@ -30,9 +31,10 @@
     return pltpu.roll(tile, shift, 1)
 
 
-def kernel(nx, ny, slot_ref, count_ref, mask_ref, params_ref, feats_ref, cot_ref, w1_ref, w2_ref,
+def kernel(nx, ny, slot_ref, count_ref, mask_ref, params_ref, feats_hbm, cot_hbm, w1_hbm, w2_hbm,
            out_ref, fg_ref, wg1_ref, wg2_ref, ng_ref,
-           rmask, field, cot, val1, val2, tmp, flat, xa, xb, xc, turned_w, f1_ref, f2_ref, halo, packs, stat_src, stats,
+           feats_ref, cot_ref, w1_ref, w2_ref, in_sem,
+           rmask, field, cot, val1, val2, tmp, flat, xa, xb, xc, turned_w, f1_ref, f2_ref, halo, packs, edges, halo_in, packs_in, stat_src, stats,
            grad, parts, share, full,
            halo_send, halo_recv, stat_send, stat_recv, rs_send, rs_recv, ag_send, ag_recv):
     group = nx * ny
@@ -49,6 +51,10 @@
             return carry
         lax.fori_loop(1, group, step, 0)
 
+    loads = [pltpu.make_async_copy(src, dst, in_sem.at[i]) for i, (src, dst) in enumerate((
+        (feats_hbm, feats_ref), (w2_hbm, w2_ref), (w1_hbm, w1_ref), (cot_hbm, cot_ref)))]
+    for load in loads:
+        load.start()
     barrier = pltpu.get_barrier_semaphore()
     each_peer(lambda j, peer: pl.semaphore_signal(
         barrier, inc=1, device_id=ident(peer), device_id_type=MESH))
@@ -93,70 +99,75 @@
 
     place(lambda k, t: jnp.broadcast_to(
         mask_ref[k:k + 1, t * 128:(t + 1) * 128].astype(F32) * live[k], (8, 128)), 8, store_mask)
+    loads[0].wait()
     place(lambda k, t: feats_ref[k, :, t * 128:(t + 1) * 128].astype(F32), C, store_input)
 
-    def halo_copy(ex, d, src):
+    planes_of = [field.at[0], val1, val2, tmp.at[1], tmp.at[2]]
+    rows_in = [C, TALL, C, C, C]
+
+    def landing(ex, d):
+        return halo_in.at[d] if ex == 0 else halo.at[ex - 1, d, 0:rows_in[ex]]
+
+    def packed(ex, h):
+        return packs_in.at[h] if ex == 0 else packs.at[ex - 1, h, 0:rows_in[ex]]
+
+    def halo_copy(ex, d):
         dx, dy = SIDES[d]
+        if dx == 0:
+            src = packed(ex, 0 if dy == 1 else 1)
+        else:
+            src = planes_of[ex].at[PLANES - 1 if dx == 1 else 0]
         return pltpu.make_async_remote_copy(
-            src_ref=src, dst_ref=halo.at[ex, d],
+            src_ref=src, dst_ref=landing(ex, d),
             send_sem=halo_send.at[ex, d], recv_sem=halo_recv.at[ex, d],
             device_id={"gx": gx + dx, "gy": gy + dy}, device_id_type=MESH)
 
     def inside(dx, dy):
         return (gx + dx >= 0) & (gx + dx < nx) & (gy + dy >= 0) & (gy + dy < ny)
-
-    def halo_sources(ex):
-        srcs = []
-        for d, (dx, dy) in enumerate(SIDES):
-            if dx == 0:
-                srcs.append(packs.at[ex, 0 if dy == 1 else 1])
-            else:
-                srcs.append(field.at[ex, PLANES - 1 if dx == 1 else 0])
-        return srcs
 
     for d, (dx, dy) in enumerate(SIDES):
         @pl.when(jnp.logical_not(inside(-dx, -dy)))
         def _(d=d):
+            halo_in[d] = jnp.zeros((C, 128), BF16)
             for ex in range(4):
-                halo[ex, d] = jnp.zeros((C, 128), BF16)
+                halo[ex, d] = jnp.zeros((TALL, 128), F32)
 
     def send_halo(ex):
-        lane = lanes()
+        rows = rows_in[ex]
+        lane = lanes(rows)
 
         def pack(i, carry):
             high, low = carry
-            plane = field[ex, i].astype(F32)
+            plane = planes_of[ex][i].astype(F32)
             here = (lane >= i * 8) & (lane < i * 8 + 8)
             high = jnp.where(here, roll(plane, lax.rem(i * 8 + 8, 128)), high)
             low = jnp.where(here, roll(plane, i * 8), low)
             return high, low
 
-        zero = jnp.zeros((C, 128), F32)
+        zero = jnp.zeros((rows, 128), F32)
         high, low = lax.fori_loop(0, PLANES, pack, (zero, zero))
-        packs[ex, 0] = high.astype(BF16)
-        packs[ex, 1] = low.astype(BF16)
-        srcs = halo_sources(ex)
+        kind = BF16 if ex == 0 else F32
+        packed(ex, 0)[...] = high.astype(kind)
+        packed(ex, 1)[...] = low.astype(kind)
         for d, (dx, dy) in enumerate(SIDES):
             @pl.when(inside(dx, dy))
             def _(d=d):
-                halo_copy(ex, d, srcs[d]).start()
+                halo_copy(ex, d).start()
 
     def wait_halo(ex):
-        srcs = halo_sources(ex)
         for d, (dx, dy) in enumerate(SIDES):
             @pl.when(inside(-dx, -dy))
             def _(d=d):
-                halo_copy(ex, d, srcs[d]).wait_recv()
+                halo_copy(ex, d).wait_recv()
 
     def done_halo(ex):
-        srcs = halo_sources(ex)
         for d, (dx, dy) in enumerate(SIDES):
             @pl.when(inside(dx, dy))
             def _(d=d):
-                halo_copy(ex, d, srcs[d]).wait_send()
-
-    def side(ex, dx, dy):
-        return halo[ex, SIDES.index((-dx, -dy))].astype(F32)
+                halo_copy(ex, d).wait_send()
+
+    def side(near, dx, dy):
+        return near[SIDES.index((-dx, -dy))].astype(F32)
 
     def spread(x, p, plane, edge):
         lane = lanes()
@@ -180,13 +191,14 @@
 
     def unfold(ex, x):
         lane = lanes()
+        near = halo_in if ex == 0 else edges
         for p, dx in ((0, -1), (PLANES + 1, 1)):
-            edge = jnp.where(lane < 64, side(ex, dx, 1), side(ex, dx, -1))
-            spread(x, p, side(ex, dx, 0), edge)
+            edge = jnp.where(lane < 64, side(near, dx, 1), side(near, dx, -1))
+            spread(x, p, side(near, dx, 0), edge)
 
         def body(i, carry):
-            before = roll(side(ex, 0, -1), lax.rem(248 - i * 8, 128))
-            after = roll(side(ex, 0, 1), lax.rem(128 - i * 8, 128))
+            before = roll(side(near, 0, -1), lax.rem(248 - i * 8, 128))
+            after = roll(side(near, 0, 1), lax.rem(128 - i * 8, 128))
             spread(x, i + 1, field[ex, i].astype(F32), jnp.where(lane < 64, after, before))
             return carry
         lax.fori_loop(0, PLANES, body, 0)
@@ -284,7 +296,7 @@
         mean = total(summed) / jnp.maximum(here, 1.0)
 
         def body(i, acc):
-            centred = (val[i] - mean) * rmask[i][0:1]
+            centred = (val[i, 0:C] - mean) * rmask[i][0:1]
             return acc + centred * centred
         spread_sum = total(lax.fori_loop(0, PLANES, body, zero_tile))
         send_stats(ph, pack_columns([total(summed), spread_sum, jnp.broadcast_to(here, (C, 1))]))
@@ -306,7 +318,7 @@
     def store_conv(val):
         def store(p, tile, acc):
             y = tile * rmask[p][0:1]
-            val[p] = y
+            val[p, 0:C] = y
             return acc + y
         return store
 
@@ -314,34 +326,55 @@
 
     pl.semaphore_wait(barrier, group - 1)
     send_halo(0)
+
+    def mask_rows(i, carry):
+        val1[i, C:TALL] = rmask[i]
+        return carry
+    lax.fori_loop(0, PLANES, mask_rows, 0)
+    for load in loads[1:]:
+        load.wait()
     place(lambda k, t: cot_ref[k, :, t * 128:(t + 1) * 128].astype(F32), C, store_cot)
     flip(w2_ref, f2_ref)
     flip(w1_ref, f1_ref)
     wait_halo(0)
     unfold(0, xa)
     summed = run_conv(w1_ref, xa, store_conv(val1), zero_tile)
+    send_halo(1)
     mean1, inv1, per = moments(0, val1, summed)
 
+    def near_mask(d):
+        return halo[0, d, C:C + 1]
+
+    def norm_one(y, m):
+        return (y - mean1) * m * inv1
+
+    def active(y, m):
+        z = norm_one(y, m) * gain1 + shift1
+        return (z * jax.nn.sigmoid(z) * m).astype(BF16)
+
     def act_one(i, carry):
-        m = rmask[i][0:1]
-        normed = (val1[i] - mean1) * m * inv1
-        val1[i] = normed
-        z = normed * gain1 + shift1
-        field[1, i] = (z * jax.nn.sigmoid(z) * m).astype(BF16)
+        field[1, i] = active(val1[i, 0:C], rmask[i][0:1])
         return carry
     lax.fori_loop(0, PLANES, act_one, 0)
-
-    send_halo(1)
     wait_halo(1)
+
+    def edge_one(d, carry):
+        edges[d] = active(halo[0, d, 0:C], near_mask(d))
+        return carry
+    lax.fori_loop(0, 8, edge_one, 0)
+
     unfold(1, xb)
     summed = run_conv(w2_ref, xb, store_conv(val2), zero_tile)
+    send_halo(2)
     mean2, inv2, per = moments(1, val2, summed)
+
+    def norm_two(y, m):
+        return (y - mean2) * m * inv2
 
     def act_two(i, carry):
         a, b = carry
         m = rmask[i][0:1]
-        normed = (val2[i] - mean2) * m * inv2
-        val2[i] = normed
+        normed = norm_two(val2[i], m)
         z = normed * gain2 + shift2
         sigma = jax.nn.sigmoid(z)
         tmp[0, i] = z * sigma * m
@@ -360,22 +393,31 @@
         ng_ref[row + 1:row + 2, :] = sums[0:1, 0:C]
         return to_columns([sums[0:1], sums[1:2]])
 
-    def back(ex, val, gz_slot, gain, inv, sums):
+    def back(ex, val, gz_slot, near_val, norm, gain, inv, sums):
         sg, gg = sums[0] * per, sums[1] * per
         scaled = gain * inv
 
+        def slope(gz, y, m):
+            return (m * scaled * (gz - sg - norm(y, m) * gg)).astype(BF16)
+
         def body(i, carry):
-            g = rmask[i][0:1] * scaled * (tmp[gz_slot, i] - sg - val[i] * gg)
-            g = g.astype(BF16)
+            g = slope(tmp[gz_slot, i], val[i, 0:C], rmask[i][0:1])
             field[ex, i] = g
             flat[:, pl.ds(pl.multiple_of(i * 128, 128), 128)] = g
             return carry
         lax.fori_loop(0, PLANES, body, 0)
+        wait_halo(ex + 1)
+
+        def edge(d, carry):
+            edges[d] = slope(halo[ex, d, 0:C], halo[near_val, d, 0:C], near_mask(d))
+            return carry
+        lax.fori_loop(0, 8, edge, 0)
 
     send_back(2, sg, gg)
+    send_halo(3)
     take(tmp.at[0], out_ref)
-    back(2, val2, 1, gain2, inv2, finish_back(2, 2))
-    send_halo(2)
+    wait_halo(2)
+    back(2, val2, 1, 1, norm_two, gain2, inv2, finish_back(2, 2))
 
     def kernel_grad(w, x):
         for lo, hi in slabs():
@@ -427,38 +469,37 @@
 
     kernel_grad(1, xb)
     start_rs(1)
-    wait_halo(2)
     unfold(2, xc)
 
     def store_gz(p, tile, carry):
         a, b = carry
-        normed = val1[p]
+        normed = norm_one(val1[p, 0:C], rmask[p][0:1])
         z = normed * gain1 + shift1
         gz = tile * rmask[p][0:1] * silu_slope(z)
-        tmp[0, p] = gz
+        tmp[2, p] = gz
         return a + gz, b + gz * normed
     sg, gg = run_conv(f2_ref, xc, store_gz, (zero_tile, zero_tile))
     send_back(3, sg, gg)
+    send_halo(4)
     finish_rs(1)
-    back(3, val1, 0, gain1, inv1, finish_back(3, 0))
-    send_halo(3)
+    back(3, val1, 2, 0, norm_one, gain1, inv1, finish_back(3, 0))
     kernel_grad(0, xa)
     start_rs(0)
-    wait_halo(3)
     unfold(3, xc)
 
     def store_fg(p, tile, carry):
-        tmp[1, p] = tile * rmask[p][0:1]
+        tmp[0, p] = tile * rmask[p][0:1]
         return carry
     run_conv(f1_ref, xc, store_fg, 0)
-    take(tmp.at[1], fg_ref)
+    take(tmp.at[0], fg_ref)
     finish_ag(1, wg2_ref)
     finish_rs(0)
     finish_ag(0, wg1_ref)
 
-    for ex in range(4):
+    for ex in range(5):
         done_halo(ex)
-        done_stats(ex)
+    for ph in range(4):
+        done_stats(ph)
     for w in range(2):
         each_peer(lambda j, peer: rs_copy(w, j, peer, me).wait_send())
         each_peer(lambda j, peer: ag_copy(w, j, peer, me).wait_send())
@@ -482,15 +523,20 @@
     return pl.pallas_call(
         functools.partial(kernel, nx, ny),
         out_shape=shapes,
-        in_specs=[smem, smem] + [vmem] * 6,
+        in_specs=[smem, smem] + [vmem] * 2 + [pl.BlockSpec(memory_space=pl.ANY)] * 4,
         out_specs=[vmem] * 5,
         scratch_shapes=[
+            pltpu.VMEM((2, C, 512), BF16),
+            pltpu.VMEM((2, C, 512), BF16),
+            pltpu.VMEM((C, COLS), BF16),
+            pltpu.VMEM((C, COLS), BF16),
+            dma((4,)),
             pltpu.VMEM((PLANES, 8, 128), F32),
             pltpu.VMEM((4, PLANES, C, 128), BF16),
             pltpu.VMEM((PLANES, C, 128), BF16),
+            pltpu.VMEM((PLANES, TALL, 128), F32),
             pltpu.VMEM((PLANES, C, 128), F32),
-            pltpu.VMEM((PLANES, C, 128), F32),
-            pltpu.VMEM((2, PLANES, C, 128), F32),
+            pltpu.VMEM((3, PLANES, C, 128), F32),
             pltpu.VMEM((C, PLANES * 128), BF16),
             pltpu.VMEM((9 * C, wide), BF16),
             pltpu.VMEM((9 * C, wide), BF16),
@@ -498,21 +544,24 @@
             pltpu.VMEM((21 * 128, 128), F32),
             pltpu.VMEM((C, 21 * 128), BF16),
             pltpu.VMEM((C, 21 * 128), BF16),
-            pltpu.VMEM((4, 8, C, 128), BF16),
-            pltpu.VMEM((4, 2, C, 128), BF16),
+            pltpu.VMEM((4, 8, TALL, 128), F32),
+            pltpu.VMEM((4, 2, TALL, 128), F32),
+            pltpu.VMEM((8, C, 128), BF16),
+            pltpu.VMEM((8, C, 128), BF16),
+            pltpu.VMEM((2, C, 128), BF16),
             pltpu.VMEM((4, 8, 128), F32),
             pltpu.VMEM((4, group, 8, 128), F32),
             pltpu.VMEM((2, GROWS, 128), BF16),
             pltpu.VMEM((2, group, GROWS // group, 128), BF16),
             pltpu.VMEM((2, GROWS // group, 128), BF16),
             pltpu.VMEM((2, GROWS, 128), BF16),
-            dma((4, 8)), dma((4, 8)),
+            dma((5, 8)), dma((5, 8)),
             dma((4, group)), dma((4, group)),
             dma((2, group)), dma((2, group)),
             dma((2, group)), dma((2, group)),
         ],
         compiler_params=pltpu.CompilerParams(
-            collective_id=0, has_side_effects=True, vmem_limit_bytes=48 * 1024 * 1024),
+            collective_id=0, has_side_effects=True, vmem_limit_bytes=60 * 1024 * 1024),
         name="section",
     )(block_slot, block_count, voxel_mask, params, feats, cotangent,
       weight_one, weight_two)

time: 120 us -> 123 us (1.025)
  Pallas kernels: 110 us -> 113 us
  local copies, waits for them, and re-layouts: 9.09 us -> 6.89 us
    pallas_call x1, Pallas kernels: 110 us -> 113 us  [per_device(): pl.pallas_call(functools.partial(kernel, nx, ny), out_shape=shapes, in_sp...]
    unnamed x25 -> x19, local copies, waits for them, and re-layouts: 9.09 us -> 6.89 us
where the time goes in v3:
time: 123 us; the launch traced here: 122 us
  Pallas kernels  113 us (92%)
  local copies, waits for them, and re-layouts  6.89 us (6%)
  between operations  1.33 us (1%)
    pallas_call x1, Pallas kernels, per_device(): pl.pallas_call(functools.partial(kernel, nx, ny), out_shape=shapes, in_sp...  113 us
    unnamed x19, local copies, waits for them, and re-layouts  6.89 us

profile of v3, /device:TPU:11, one launch (start us, length us, event | category | flops | bytes accessed | tf_op | source)
XLA Modules:
  0.0 121.7 jit_solution(2698736479127956069)
XLA Ops:
  1.3 0.0 copy-start.6
  1.3 0.0 copy-start.3
  1.3 0.0 copy-start.4
  1.3 0.0 copy-start.5
  1.3 0.6 copy-done.6
  1.9 0.0 copy-done.3
  2.0 0.0 copy-done.4
  2.0 0.0 copy-done.5
  2.0 0.6 select_maximum_fusion.params_ref
  2.6 112.9 %section.1 = (bf16[2,96,512]{2,1,0:T(8,128)(2,1)}, bf16[2,96,512]{2,1,0:T(8,128)(2,1)}, f32[96,2592]{1,0:T(8,128)}, f32[96,2592]{1,0:T(8,128)}, f32[4,96]{1,0:T(4,128)}) custom-call(s32[2]{0:T(128)} %slot_ref.1, s32[1]{0:T(128)S(6)} %copy.21.count_ref, s32[2,512]{1,0:T(2,128)} %mask_ref.1, f32[8,128]{1,0:T(8,128)} %select_maximum_fusion.params_ref, ...), custom_call_target="tpu_custom_call" | custom-call | tf_op jit(solution)/shard_map/section/pallas_call | solution.py:523
  115.5 0.0 copy-start.1
  115.5 1.7 %copy.22 = bf16[2,96,512]{2,1,0:T(8,128)(2,1)} copy(bf16[2,96,512]{2,1,0:T(8,128)(2,1)} %get-tuple-element.10) | data formatting | bytes 393216
  117.2 0.0 copy-done.1
  117.2 0.7 copy.23
  117.9 0.0 copy-start
  117.9 2.3 %copy.24 = f32[96,2592]{1,0:T(8,128)} copy(f32[96,2592]{1,0:T(8,128)} %get-tuple-element.12) | data formatting | bytes 1990656
  120.2 0.0 copy-done
  120.2 0.0 copy-start.2
  120.2 1.0 copy.25
  121.2 0.0 copy-done.2
  121.2 0.6 copy.26
Async XLA Ops:
  1.3 0.7 copy-start.6
  1.3 0.7 copy-start.3
  1.3 0.7 copy-start.4
  1.3 0.7 copy-start.5
  115.5 1.7 %copy-start.1 = (bf16[2,96,512]{2,1,0:T(8,128)(2,1)S(1)}, bf16[2,96,512]{2,1,0:T(8,128)(2,1)}, u32[]{:S(2)}) copy-start(bf16[2,96,512]{2,1,0:T(8,128)(2,1)} %get-tuple-element.11) | copy-start | bytes 589828
  117.9 2.3 %copy-start = (f32[96,2592]{1,0:T(8,128)S(1)}, f32[96,2592]{1,0:T(8,128)}, u32[]{:S(2)}) copy-start(f32[96,2592]{1,0:T(8,128)} %get-tuple-element.13) | copy-start | bytes 2985988
  120.2 1.0 copy-start.2

commit v4 on v3

--- a/solution.py
+++ b/solution.py
@@ -34,7 +34,7 @@
 def kernel(nx, ny, slot_ref, count_ref, mask_ref, params_ref, feats_hbm, cot_hbm, w1_hbm, w2_hbm,
            out_ref, fg_ref, wg1_ref, wg2_ref, ng_ref,
            feats_ref, cot_ref, w1_ref, w2_ref, in_sem,
-           rmask, field, cot, val1, val2, tmp, flat, xa, xb, xc, turned_w, f1_ref, f2_ref, halo, packs, edges, halo_in, packs_in, stat_src, stats,
+           rmask, field, cot, val1, val2, tmp, flat, xa, xb, xc, turned_w, f1_ref, f2_ref, halo, packs, edges, halo_in, packs_in, corner_src, corner_in, stat_src, stats,
            grad, parts, share, full,
            halo_send, halo_recv, stat_send, stat_recv, rs_send, rs_recv, ag_send, ag_recv):
     group = nx * ny
@@ -106,6 +106,8 @@
     rows_in = [C, TALL, C, C, C]
 
     def landing(ex, d):
+        if d >= 4:
+            return corner_in.at[ex, d - 4]
         return halo_in.at[d] if ex == 0 else halo.at[ex - 1, d, 0:rows_in[ex]]
 
     def packed(ex, h):
@@ -113,7 +115,9 @@
 
     def halo_copy(ex, d):
         dx, dy = SIDES[d]
-        if dx == 0:
+        if d >= 4:
+            src = corner_src.at[ex, d - 4]
+        elif dx == 0:
             src = packed(ex, 0 if dy == 1 else 1)
         else:
             src = planes_of[ex].at[PLANES - 1 if dx == 1 else 0]
@@ -128,6 +132,10 @@
     for d, (dx, dy) in enumerate(SIDES):
         @pl.when(jnp.logical_not(inside(-dx, -dy)))
         def _(d=d):
+            if d >= 4:
+                for ex in range(5):
+                    corner_in[ex, d - 4] = jnp.zeros((8, 128), F32)
+                return
             halo_in[d] = jnp.zeros((C, 128), BF16)
             for ex in range(4):
                 halo[ex, d] = jnp.zeros((TALL, 128), F32)
@@ -136,16 +144,20 @@
         rows = rows_in[ex]
         lane = lanes(rows)
 
-        def pack(i, carry):
-            high, low = carry
+        for dx in (1, -1):
+            plane = planes_of[ex][PLANES - 1 if dx == 1 else 0].astype(F32)
+            turned = jnp.transpose(jnp.concatenate(
+                [plane, jnp.zeros((128 - rows, 128), F32)], axis=0))
+            corner_src[ex, SIDES.index((dx, 1)) - 4] = turned[120:128]
+            corner_src[ex, SIDES.index((dx, -1)) - 4] = turned[0:8]
+
+        high = low = jnp.zeros((rows, 128), F32)
+        for i in range(PLANES):
             plane = planes_of[ex][i].astype(F32)
             here = (lane >= i * 8) & (lane < i * 8 + 8)
-            high = jnp.where(here, roll(plane, lax.rem(i * 8 + 8, 128)), high)
-            low = jnp.where(here, roll(plane, i * 8), low)
-            return high, low
-
-        zero = jnp.zeros((rows, 128), F32)
-        high, low = lax.fori_loop(0, PLANES, pack, (zero, zero))
+            to_high, to_low = (i * 8 + 8) % 128, i * 8
+            high = jnp.where(here, roll(plane, to_high) if to_high else plane, high)
+            low = jnp.where(here, roll(plane, to_low) if to_low else plane, low)
         kind = BF16 if ex == 0 else F32
         packed(ex, 0)[...] = high.astype(kind)
         packed(ex, 1)[...] = low.astype(kind)
@@ -159,6 +171,15 @@
             @pl.when(inside(-dx, -dy))
             def _(d=d):
                 halo_copy(ex, d).wait_recv()
+        for slot, dx in ((4, -1), (5, 1)):
+            after = corner_in[ex, SIDES.index((-dx, -1)) - 4]
+            before = corner_in[ex, SIDES.index((-dx, 1)) - 4]
+            tile = jnp.transpose(jnp.concatenate(
+                [after, jnp.zeros((112, 128), F32), before], axis=0))
+            if ex == 0:
+                halo_in[slot] = tile[0:C].astype(BF16)
+            else:
+                halo[ex - 1, slot] = tile[0:TALL]
 
     def done_halo(ex):
         for d, (dx, dy) in enumerate(SIDES):
@@ -193,7 +214,7 @@
         lane = lanes()
         near = halo_in if ex == 0 else edges
         for p, dx in ((0, -1), (PLANES + 1, 1)):
-            edge = jnp.where(lane < 64, side(near, dx, 1), side(near, dx, -1))
+            edge = near[4 if dx == -1 else 5].astype(F32)
             spread(x, p, side(near, dx, 0), edge)
 
         def body(i, carry):
@@ -361,7 +382,7 @@
     def edge_one(d, carry):
         edges[d] = active(halo[0, d, 0:C], near_mask(d))
         return carry
-    lax.fori_loop(0, 8, edge_one, 0)
+    lax.fori_loop(0, 6, edge_one, 0)
 
     unfold(1, xb)
     summed = run_conv(w2_ref, xb, store_conv(val2), zero_tile)
@@ -411,7 +432,7 @@
         def edge(d, carry):
             edges[d] = slope(halo[ex, d, 0:C], halo[near_val, d, 0:C], near_mask(d))
             return carry
-        lax.fori_loop(0, 8, edge, 0)
+        lax.fori_loop(0, 6, edge, 0)
 
     send_back(2, sg, gg)
     send_halo(3)
@@ -549,6 +570,8 @@
             pltpu.VMEM((8, C, 128), BF16),
             pltpu.VMEM((8, C, 128), BF16),
             pltpu.VMEM((2, C, 128), BF16),
+            pltpu.VMEM((5, 4, 8, 128), F32),
+            pltpu.VMEM((5, 4, 8, 128), F32),
             pltpu.VMEM((4, 8, 128), F32),
             pltpu.VMEM((4, group, 8, 128), F32),
             pltpu.VMEM((2, GROWS, 128), BF16),

time: 123 us -> 115 us (0.935)
  Pallas kernels: 113 us -> 104 us
    pallas_call x1, Pallas kernels: 113 us -> 104 us  [per_device(): pl.pallas_call(functools.partial(kernel, nx, ny), out_shape=shapes, in_sp...]
where the time goes in v4:
time: 115 us; the launch traced here: 113 us
  Pallas kernels  104 us (90%)
  local copies, waits for them, and re-layouts  6.89 us (6%)
  between operations  1.33 us (1%)
    pallas_call x1, Pallas kernels, per_device(): pl.pallas_call(functools.partial(kernel, nx, ny), out_shape=shapes, in_sp...  104 us
    unnamed x19, local copies, waits for them, and re-layouts  6.89 us

profile of v4, /device:TPU:11, one launch (start us, length us, event | category | flops | bytes accessed | tf_op | source)
XLA Modules:
  0.0 113.1 jit_solution(3842283512298180072)
XLA Ops:
  1.3 0.0 copy-start.6
  1.3 0.0 copy-start.3
  1.3 0.0 copy-start.4
  1.3 0.0 copy-start.5
  1.3 0.6 copy-done.6
  1.9 0.0 copy-done.3
  2.0 0.0 copy-done.4
  2.0 0.0 copy-done.5
  2.0 0.6 select_maximum_fusion.params_ref
  2.6 104.2 %section.1 = (bf16[2,96,512]{2,1,0:T(8,128)(2,1)}, bf16[2,96,512]{2,1,0:T(8,128)(2,1)}, f32[96,2592]{1,0:T(8,128)}, f32[96,2592]{1,0:T(8,128)}, f32[4,96]{1,0:T(4,128)}) custom-call(s32[2]{0:T(128)} %slot_ref.1, s32[1]{0:T(128)S(6)} %copy.21.count_ref, s32[2,512]{1,0:T(2,128)} %mask_ref.1, f32[8,128]{1,0:T(8,128)} %select_maximum_fusion.params_ref, ...), custom_call_target="tpu_custom_call" | custom-call | tf_op jit(solution)/shard_map/section/pallas_call | solution.py:544
  106.8 0.0 copy-start.1
  106.9 1.7 %copy.22 = bf16[2,96,512]{2,1,0:T(8,128)(2,1)} copy(bf16[2,96,512]{2,1,0:T(8,128)(2,1)} %get-tuple-element.10) | data formatting | bytes 393216
  108.5 0.0 copy-done.1
  108.5 0.7 copy.23
  109.2 0.0 copy-start
  109.2 2.3 %copy.24 = f32[96,2592]{1,0:T(8,128)} copy(f32[96,2592]{1,0:T(8,128)} %get-tuple-element.12) | data formatting | bytes 1990656
  111.5 0.0 copy-done
  111.5 0.0 copy-start.2
  111.5 1.0 copy.25
  112.5 0.0 copy-done.2
  112.5 0.6 copy.26
Async XLA Ops:
  1.3 0.7 copy-start.6
  1.3 0.7 copy-start.3
  1.3 0.7 copy-start.4
  1.3 0.7 copy-start.5
  106.8 1.7 %copy-start.1 = (bf16[2,96,512]{2,1,0:T(8,128)(2,1)S(1)}, bf16[2,96,512]{2,1,0:T(8,128)(2,1)}, u32[]{:S(2)}) copy-start(bf16[2,96,512]{2,1,0:T(8,128)(2,1)} %get-tuple-element.11) | copy-start | bytes 589828
  109.2 2.3 %copy-start = (f32[96,2592]{1,0:T(8,128)S(1)}, f32[96,2592]{1,0:T(8,128)}, u32[]{:S(2)}) copy-start(f32[96,2592]{1,0:T(8,128)} %get-tuple-element.13) | copy-start | bytes 2985988
  111.5 1.0 copy-start.2
